TPU v7x, 256 devices: a whole 4x4x8 slice. The times are simulated.
256 devices in a mesh: dp: 32 (over x, y, core), mp: 8 (over z).
Axes of the slice: x: 4, y: 4, z: 8, core: 2. Of those that a mesh axis runs over, the one named last changes fastest.
Arguments:
- hidden_first: bfloat16 [6144, 4096], P('dp'), may hold values from -256 to 256, as said below
- hidden_second: bfloat16 [6144, 4096], P('dp'), may hold values from -256 to 256, as said below
- weight: bfloat16 [4096, 4096], P('dp', 'mp'), may hold values from -0.09375 to 0.09375
Outputs:
- grad_weight: bfloat16 [4096, 4096], P('dp', 'mp')
- grad_first: bfloat16 [6144, 4096], P('dp', 'mp')
- grad_second: bfloat16 [6144, 4096], P('dp', 'mp')
Inputs may be any that keep to these rules, and one draw needn't show every extreme that they name: `hidden_first`: hidden activations of two augmented views of the same molecules. `hidden_second`: hidden activations of two augmented views of the same molecules.
All inputs are finite; a program needn't handle non-finite values.
Results may differ from a plain program's by a relative error of at most 0.023.
Values may be sent and summed in bfloat16 or wider, within the bound.
A program may use at most 64 MiB of HBM per device.

v0:
```python
import math

import jax
import jax.numpy as jnp
from jax import lax
from jax.sharding import PartitionSpec as P

epsilon = 1e-05
offdiag_weight = 0.0051


def contract_lead(left, right):
    return lax.dot_general(
        left, right, (((0,), (0,)), ((), ())), preferred_element_type=jnp.float32
    )


def contract_tail(left, right):
    return lax.dot_general(
        left, right, (((1,), (1,)), ((), ())), preferred_element_type=jnp.float32
    )


def local(hidden_first, hidden_second, weight):
    rows = hidden_first.shape[0]
    columns = weight.shape[1]
    total_rows = rows * lax.axis_size("dp")
    full_weight = lax.all_gather(weight, "dp", axis=0, tiled=True)
    project_first = jnp.dot(hidden_first, full_weight, preferred_element_type=jnp.float32)
    project_second = jnp.dot(hidden_second, full_weight, preferred_element_type=jnp.float32)
    projected = jnp.stack([project_first, project_second])
    center = lax.psum(jnp.sum(projected, axis=1), "dp") / total_rows
    shifted = projected - center[:, None, :]
    variance = lax.psum(jnp.sum(shifted * shifted, axis=1), "dp") / total_rows
    spread = jnp.sqrt(variance + epsilon)[:, None, :]
    normed = ((projected - center[:, None, :]) / spread).astype(jnp.bfloat16)
    norm_first = normed[0]
    all_second = lax.all_gather(normed[1], "mp", axis=1, tiled=True)
    block_rows = all_second.shape[1] // lax.axis_size("dp")
    block = all_second
    crossed = (
        lax.psum_scatter(
            contract_lead(block, norm_first).astype(jnp.bfloat16),
            "dp",
            scatter_dimension=0,
            tiled=True,
        ).astype(jnp.float32)
        / total_rows
    )
    second_index = lax.axis_index("dp") * block_rows + lax.broadcasted_iota(
        jnp.int32, crossed.shape, 0
    )
    first_index = lax.axis_index("mp") * columns + lax.broadcasted_iota(jnp.int32, crossed.shape, 1)
    loss_grad = jnp.where(
        second_index == first_index, 2.0 * (crossed - 1.0), 2.0 * offdiag_weight * crossed
    ).astype(jnp.bfloat16)
    all_grad = lax.all_gather(loss_grad, "dp", axis=0, tiled=True)
    upstream_first = jnp.dot(all_second, all_grad, preferred_element_type=jnp.float32)
    block = all_grad
    upstream_second = (
        lax.psum_scatter(
            contract_tail(block, norm_first).astype(jnp.bfloat16),
            "mp",
            scatter_dimension=0,
            tiled=True,
        )
        .astype(jnp.float32)
        .T
    )
    upstream = jnp.stack([upstream_first, upstream_second])
    normed_float = normed.astype(jnp.float32)
    level_sums, slope_sums = lax.psum(
        (jnp.sum(upstream, axis=1), jnp.sum(upstream * normed_float, axis=1)), "dp"
    )
    level = (level_sums / total_rows)[:, None, :]
    slope = (slope_sums / total_rows)[:, None, :]
    down = ((upstream - level - normed_float * slope) / spread).astype(jnp.bfloat16)
    stacked_down = down.reshape(2 * rows, columns)
    partial_hidden = contract_tail(stacked_down, full_weight)
    hidden_grads = lax.psum_scatter(
        partial_hidden.astype(jnp.bfloat16), "mp", scatter_dimension=1, tiled=True
    )
    summed_weight = lax.psum_scatter(
        (contract_lead(hidden_first, down[0]) + contract_lead(hidden_second, down[1])).astype(
            jnp.bfloat16
        ),
        "dp",
        scatter_dimension=0,
        tiled=True,
    ).astype(jnp.float32)
    grad_weight = (summed_weight / math.sqrt(total_rows)).astype(jnp.bfloat16)
    return (grad_weight, hidden_grads[:rows], hidden_grads[rows:])


def solution(mesh):
    in_specs = (P("dp", None), P("dp", None), P("dp", "mp"))
    out_specs = (P("dp", "mp"), P("dp", "mp"), P("dp", "mp"))
    return jax.shard_map(local, mesh=mesh, in_specs=in_specs, out_specs=out_specs, check_vma=False)
```

profile of v0, /device:TPU:6, one launch (start us, length us, event | category | flops | bytes accessed | tf_op | source)
XLA Modules:
  0.0 646.4 jit_solution(1856966342831952057)
XLA Ops:
  7.2 0.0 all-gather.5.cloned.1.call-start
  7.2 0.7 all-gather.5.cloned.1.call-update
  7.9 0.0 all-gather.9.cloned.1.call-start
  8.0 56.3 %all-gather.5.cloned.1.call-done = bf16[4096,512]{1,0:T(8,128)(2,1)} async-done(((bf16[128,512]{1,0:T(8,128)(2,1)}), bf16[4096,512]{1,0:T(8,128)(2,1)}) %all-gather.5.cloned.1.call-update) | async-done | bytes 4194320 | tf_op jit(solution)/shard_map/all_gather | solution.py:28
  64.3 3.8 convolution_bitcast_fusion
  68.1 0.1 copy-done.1
  68.1 1.0 convolution_bitcast_fusion.1
  69.2 0.1 fusion.15
  69.2 54.3 %psum.28 = f32[2,512]{1,0:T(2,128)S(1)} all-reduce(f32[2,512]{1,0:T(2,128)S(1)} %fusion.15), channel_id=1, replica_groups=mesh['dp'=32,'mp'=8] {'dp'}, use_global_device_ids=true, to_apply=%region_1.0 | all-reduce | flops 1024 | bytes 8192 | tf_op jit(solution)/shard_map/psum | solution.py:32
  123.5 0.1 multiply_reduce_fusion
  123.7 56.1 %psum.29 = f32[2,512]{1,0:T(2,128)S(1)} all-reduce(f32[2,512]{1,0:T(2,128)S(1)} %get-tuple-element.15), channel_id=1, replica_groups=mesh['dp'=32,'mp'=8] {'dp'}, use_global_device_ids=true, to_apply=%region_3.0 | all-reduce | flops 1024 | bytes 8192 | tf_op jit(solution)/shard_map/psum | solution.py:34
  179.8 0.1 divide_convert_fusion
  179.8 0.7 slice.24
  180.5 0.0 all-gather.9.cloned.1.call-update
  180.6 0.0 reduce-scatter.7.cloned.1.call-start
  180.6 54.4 %all-gather.9.cloned.1.call-done = bf16[1,192,4096]{2,1,0:T(8,128)(2,1)} async-done(((bf16[1,192,512]{2,1,0:T(8,128)(2,1)}), bf16[1,192,4096]{2,1,0:T(8,128)(2,1)}) %all-gather.9.cloned.1.call-update) | async-done | bytes 1572880 | tf_op jit(solution)/shard_map/all_gather | solution.py:38
  235.0 4.7 convolution_convert_fusion
  239.7 0.0 reduce-scatter.7.cloned.1.call-update
  239.7 0.0 all-gather.7.cloned.1.call-start
  239.8 88.0 %reduce-scatter.7.cloned.1.call-done = bf16[128,512]{1,0:T(8,128)(2,1)} async-done(((bf16[4096,512]{1,0:T(8,128)(2,1)}), bf16[128,512]{1,0:T(8,128)(2,1)}) %reduce-scatter.7.cloned.1.call-update) | async-done | bytes 131088 | tf_op jit(solution)/shard_map/reduce_scatter | solution.py:42
  327.8 1.6 fusion.21
  329.4 0.0 all-gather.7.cloned.1.call-update
  329.4 0.0 reduce-scatter.9.cloned.1.call-start
  329.5 52.1 %all-gather.7.cloned.1.call-done = bf16[4096,512]{1,0:T(8,128)(2,1)} async-done(((bf16[128,512]{1,0:T(8,128)(2,1)}), bf16[4096,512]{1,0:T(8,128)(2,1)}) %all-gather.7.cloned.1.call-update) | async-done | bytes 4194320 | tf_op jit(solution)/shard_map/all_gather | solution.py:57
  381.6 4.9 convolution_convert_fusion.2
  386.4 0.0 reduce-scatter.9.cloned.1.call-update
  386.4 0.0 reduce-scatter.13.cloned.1.call-start
  386.5 3.6 fusion.4
  390.2 36.7 %reduce-scatter.9.cloned.1.call-done = bf16[512,192]{0,1:T(8,128)(2,1)} async-done(((bf16[4096,192]{0,1:T(8,128)(2,1)}), bf16[512,192]{0,1:T(8,128)(2,1)}) %reduce-scatter.9.cloned.1.call-update) | async-done | bytes 196624 | tf_op jit(solution)/shard_map/reduce_scatter | solution.py:61
  426.8 1.0 convert_bitcast_fusion
  427.8 0.2 fusion.7
  428.0 54.0 %all-reduce = (f32[2,512]{1,0:T(2,128)S(1)}, f32[2,512]{1,0:T(2,128)S(1)}) all-reduce(f32[2,512]{1,0:T(2,128)S(1)} %get-tuple-element.10, f32[2,512]{1,0:T(2,128)S(1)} %get-tuple-element.9), channel_id=1, replica_groups=mesh['dp'=32,'mp'=8] {'dp'}, use_global_device_ids=true, to_apply=%region_7.8 | all-reduce | flops 2048 | bytes 16384 | tf_op jit(solution)/shard_map/psum | solution.py:72
  482.0 1.1 fusion.10
  483.2 1.3 fusion.22
  484.5 0.1 copy-done.2
  484.6 3.3 fusion
  487.9 6.5 %copy.8 = bf16[4096,512]{1,0:T(8,128)(2,1)} copy(bf16[4096,512]{0,1:T(8,128)(2,1)} %fusion) | data formatting | bytes 8388608
  494.4 0.0 reduce-scatter.13.cloned.1.call-update
  494.4 0.0 reduce-scatter.11.cloned.1.call-start
  494.5 1.1 copy-done.3
  495.5 0.2 fusion.12
  495.7 5.8 convolution_convert_fusion.1
  501.5 0.0 reduce-scatter.11.cloned.1.call-update
  501.5 87.0 %reduce-scatter.13.cloned.1.call-done = bf16[128,512]{1,0:T(8,128)(2,1)} async-done(((bf16[4096,512]{1,0:T(8,128)(2,1)}), bf16[128,512]{1,0:T(8,128)(2,1)}) %reduce-scatter.13.cloned.1.call-update) | async-done | bytes 131088
  588.5 1.0 copy.9
  589.5 0.8 copy.7
  590.3 47.4 %reduce-scatter.11.cloned.1.call-done = bf16[384,512]{1,0:T(8,128)(2,1)} async-done(((bf16[384,4096]{1,0:T(8,128)(2,1)}), bf16[384,512]{1,0:T(8,128)(2,1)}) %reduce-scatter.11.cloned.1.call-update) | async-done | bytes 393232 | tf_op jit(solution)/shard_map/reduce_scatter | solution.py:80
  637.8 1.8 fusion.25
  (11 shorter events, 0.1 us)
Async XLA Ops:
  7.2 60.9 %copy-start = (bf16[192,4096]{1,0:T(8,128)(2,1)S(1)}, bf16[192,4096]{1,0:T(8,128)(2,1)}, u32[]{:S(2)}) copy-start(bf16[192,4096]{1,0:T(8,128)(2,1)} %param.3) | copy-start | bytes 4718596
  7.2 57.1 %all-gather.5.cloned.1.call-start = ((), (), s32[]{:S(2)}) async-start(), calls=%async_computation.4 | async-start | bytes 4325376 | tf_op jit(solution)/shard_map/all_gather | solution.py:28
  7.9 227.1 %all-gather.9.cloned.1.call-start = ((), (), s32[]{:S(2)}) async-start(), calls=%async_computation.9 | async-start | bytes 1769472 | tf_op jit(solution)/shard_map/all_gather | solution.py:38
  64.3 3.9 copy-start.1
  180.6 147.2 %reduce-scatter.7.cloned.1.call-start = ((), (), s32[]{:S(2)}) async-start(), calls=%async_computation.5 | async-start | bytes 4325376 | tf_op jit(solution)/shard_map/reduce_scatter | solution.py:42
  239.7 141.9 %all-gather.7.cloned.1.call-start = ((), (), s32[]{:S(2)}) async-start(), calls=%async_computation.6 | async-start | bytes 4325376 | tf_op jit(solution)/shard_map/all_gather | solution.py:57
  329.4 97.4 %reduce-scatter.9.cloned.1.call-start = ((), (), s32[]{:S(2)}) async-start(), calls=%async_computation.7 | async-start | bytes 1769472 | tf_op jit(solution)/shard_map/reduce_scatter | solution.py:61
  386.4 202.0 %reduce-scatter.13.cloned.1.call-start = ((), (), s32[]{:S(2)}) async-start(), calls=%async_computation.10 | async-start | bytes 4325376
  483.2 1.4 copy-start.2
  494.4 1.1 copy-start.3
  494.4 143.3 %reduce-scatter.11.cloned.1.call-start = ((), (), s32[]{:S(2)}) async-start(), calls=%async_computation.8 | async-start | bytes 3538944 | tf_op jit(solution)/shard_map/reduce_scatter | solution.py:80
Sparse Core Ops, SparseCore 0:
  10.6 53.6 all-gather.4
  180.7 54.2 all-gather.8
  239.8 87.8 reduce-scatter.6
  331.1 50.4 all-gather.6
  386.6 40.1 reduce-scatter.8
  494.5 93.8 reduce-scatter.12
  591.0 46.6 reduce-scatter.10
where the time goes:
time: 647 us; the launch traced here: 646 us
  waiting for transfers between devices  423 us (65%)
  blocking collectives  164 us (25%)
  matrix products  28.3 us (4%)
  between operations  14.2 us (2%)
  local copies, waits for them, and re-layouts  12.1 us (2%)
    reduce_scatter x1, waiting for transfers between devices, local(): lax.psum_scatter(contract_lead(block, norm_first).astype(jnp.bfloat16), '...  88 us
    unnamed x8, waiting for transfers between devices  87.7 us
    all_gather x1, waiting for transfers between devices, local(): full_weight = lax.all_gather(weight, 'dp', axis=0, tiled=True)  56.3 us
    psum x1, blocking collectives, local(): variance = lax.psum(jnp.sum(shifted * shifted, axis=1), 'dp') / total_rows  56.1 us
    all_gather x1, waiting for transfers between devices, local(): all_second = lax.all_gather(normed[1], 'mp', axis=1, tiled=True)  54.4 us
    psum x1, blocking collectives, local(): center = lax.psum(jnp.sum(projected, axis=1), 'dp') / total_rows  54.3 us
    psum x1, blocking collectives, local(): lax.psum((jnp.sum(upstream, axis=1), jnp.sum(upstream * normed_float, axi...  54 us
    all_gather x1, waiting for transfers between devices, local(): all_grad = lax.all_gather(loss_grad, 'dp', axis=0, tiled=True)  52.1 us
  transfers between devices with their start and end apart: 7, of which 7 were waited for; matrix products, arithmetic and copies ran while one was open for 2% of the time, Pallas kernels for 0%

commit v1 on v0

v1 whole, which is shorter than its diff:
```python
import math

import jax
import jax.numpy as jnp
from jax import lax
from jax.experimental import pallas as pl
from jax.experimental.pallas import tpu as pltpu
from jax.sharding import PartitionSpec as P

MESH = pl.DeviceIdType.MESH
BF = jnp.bfloat16
F32 = jnp.float32

epsilon = 1e-05
offdiag_weight = 0.0051

TOKENS = 6144
ROWS = 192
PAD = 208
COLS = 512
NZ = 8


def wrap(value, size):
    return lax.rem(value + size, size)


class Place:
    def __init__(self):
        dp = lax.axis_index("dp")
        self.dp = dp
        self.x = lax.div(dp, 8)
        self.y = lax.rem(lax.div(dp, 2), 4)
        self.c = lax.rem(dp, 2)
        self.z = lax.axis_index("mp")

    def X(self, d):
        return wrap(self.x + d, 4)

    def Y(self, d):
        return wrap(self.y + d, 4)

    def Z(self, d):
        return wrap(self.z + d, NZ)

    def block(self, dx, dy, dc=0):
        return self.X(dx) * 8 + self.Y(dy) * 2 + wrap(self.c + dc, 2)

    def at(self, dx, dy, dc=0):
        return {"dp": self.block(dx, dy, dc)}

    def sib(self):
        return {"dp": self.dp + 1 - 2 * self.c}

    def up(self, d):
        return {"mp": self.Z(d)}

    def plane_peers(self):
        row = [(0, dy, dc) for dy in range(4) for dc in range(2)][1:]
        column = [(dx, 0, 0) for dx in range(1, 4)]
        return [self.at(*p) for p in row + column]

    def z_peers(self):
        return [self.up(d) for d in range(1, NZ)]


class Net:
    def __init__(self, sends, recvs):
        self.sends, self.recvs = sends, recvs
        self.copies = []

    def send(self, src, dst, to):
        index = len(self.copies)
        copy = pltpu.make_async_remote_copy(
            src_ref=src,
            dst_ref=dst,
            send_sem=self.sends.at[index],
            recv_sem=self.recvs.at[index],
            device_id=to,
            device_id_type=MESH,
        )
        copy.start()
        self.copies.append(copy)
        return copy

    def drain(self):
        for copy in self.copies:
            copy.wait_send()


def barrier(peers):
    sem = pltpu.get_barrier_semaphore()
    for peer in peers:
        pl.semaphore_signal(sem, inc=1, device_id=peer, device_id_type=MESH)
    pl.semaphore_wait(sem, len(peers))


def dot(a, b, dims):
    return lax.dot_general(a, b, ((dims[0], dims[1]), ((), ())), preferred_element_type=F32)


def turn(o, first, second):
    return (first, second) if o == 0 else (second, first)


def gather_plane(net, me, W):
    def block(o, a, b):
        return me.block(*turn(o, a, b))

    def to(o, a, b):
        return me.at(*turn(o, a, b))

    def push(index, start, size, target):
        ref = W.at[index, pl.ds(start, size)]
        return net.send(ref, ref, target)

    own = me.block(0, 0)
    both = [(o, d) for d in (1, -1) for o in (0, 1)]
    first, second, half, far, sibs = {}, {}, {}, {}, []

    def over(o, a):
        for d in (1, -1):
            second[o, a, d] = push(block(o, a, 0), 64 * o, 64, to(o, 0, d))

    def share(o, a, b):
        sibs.append(push(block(o, a, b), 64 * o, 64, me.sib()))

    for o, d in both:
        first[o, d] = push(own, 64 * o, 64, to(o, d, 0))
    for o in (0, 1):
        over(o, 0)
    sibs.append(net.send(W.at[own], W.at[own], me.sib()))
    for o, d in both:
        first[o, d].wait_recv()
        half[o, d] = push(block(o, -d, 0), 64 * o + (0 if d == 1 else 32), 32, to(o, d, 0))
    for o, d in both:
        over(o, -d)
    for o, d in both:
        share(o, -d, 0)
    for o in (0, 1):
        half[o, 1].wait_recv()
        half[o, -1].wait_recv()
        over(o, 2)
        share(o, 2, 0)
    for a in (0, -1, 1, 2):
        for o, d in both:
            second[o, a, d].wait_recv()
            far[o, a, d] = push(
                block(o, a, -d), 64 * o + (0 if d == 1 else 32), 32, to(o, 0, d)
            )
            share(o, a, -d)
    for a in (0, -1, 1, 2):
        for o in (0, 1):
            far[o, a, 1].wait_recv()
            far[o, a, -1].wait_recv()
            share(o, a, 2)
    for copy in sibs:
        copy.wait_recv()


def scatter_plane(net, me, S, M1, F1, Q, M2, F2):
    def index(o, d):
        return me.X(d) if o == 0 else me.Y(d)

    def other(o, d):
        return me.Y(d) if o == 0 else me.X(d)

    def part(o, d, start, size=2):
        rows = pl.ds(64 * o, 64)
        if o == 0:
            return (index(o, d), pl.ds(start, size), rows)
        return (pl.ds(start, size), index(o, d), rows)

    def to(o, a, b):
        return me.at(*turn(o, a, b))

    both = [(o, d) for d in (1, -1) for o in (0, 1)]
    slot = {1: 0, -1: 1}
    mid, early, late = {}, {}, {}
    for o, d in both:
        h = 0 if d == 1 else 2
        mid[o, d] = net.send(S.at[part(o, 2, h)], M1.at[o, slot[d]], to(o, d, 0))
    for o, d in both:
        h = 0 if d == 1 else 2
        early[o, d] = net.send(
            S.at[part(o, d, 2 - h)], F1.at[o, slot[d], pl.ds(2 - h, 2)], to(o, d, 0)
        )
    for o, d in both:
        h = 0 if d == 1 else 2
        mid[o, d].wait_recv()
        S[part(o, d, h)] += M1[o, slot[d]]
        late[o, d] = net.send(S.at[part(o, d, h)], F1.at[o, slot[d], pl.ds(h, 2)], to(o, d, 0))
    mid2, early2, late2 = {}, {}, {}
    for o in (0, 1):
        for d in (1, -1):
            early[o, d].wait_recv()
            late[o, d].wait_recv()
        total = S[part(o, 0, 0, 4)].astype(F32) + F1[o, 0].astype(F32) + F1[o, 1].astype(F32)
        Q[o] = total.astype(BF)
        for d in (1, -1):
            h = 0 if d == 1 else 32
            mid2[o, d] = net.send(
                Q.at[o, other(o, 2), pl.ds(h, 32)], M2.at[o, slot[d]], to(o, 0, d)
            )
        for d in (1, -1):
            h = 0 if d == 1 else 32
            early2[o, d] = net.send(
                Q.at[o, other(o, d), pl.ds(32 - h, 32)],
                F2.at[o, slot[d], pl.ds(32 - h, 32)],
                to(o, 0, d),
            )
    for o in (0, 1):
        for d in (1, -1):
            h = 0 if d == 1 else 32
            mid2[o, d].wait_recv()
            Q[o, other(o, d), pl.ds(h, 32)] += M2[o, slot[d]]
            late2[o, d] = net.send(
                Q.at[o, other(o, d), pl.ds(h, 32)], F2.at[o, slot[d], pl.ds(h, 32)], to(o, 0, d)
            )
    result = []
    for o in (0, 1):
        for d in (1, -1):
            early2[o, d].wait_recv()
            late2[o, d].wait_recv()
        result.append(
            Q[o, other(o, 0)].astype(F32) + F2[o, 0].astype(F32) + F2[o, 1].astype(F32)
        )
    return result


def scatter_plane_scratch():
    return [
        pltpu.VMEM((2, 2, 2, 64, COLS), BF),
        pltpu.VMEM((2, 2, 4, 64, COLS), BF),
        pltpu.VMEM((2, 4, 64, COLS), BF),
        pltpu.VMEM((2, 2, 32, COLS), BF),
        pltpu.VMEM((2, 2, 64, COLS), BF),
    ]


class ScatterZ:
    def __init__(self, net, me, T, R, rows):
        self.net, self.me, self.T, self.R = net, me, T, R
        self.half = rows // 2
        self.copies = {}

    def slice(self, half):
        return pl.ds(half * self.half, self.half)

    def send(self, d, s, half):
        slot = 0 if d == 1 else 1
        index = self.me.Z(d * (4 - s))
        rows = self.slice(half)
        previous = self.copies.get((d, s - 1, half))
        if previous is not None:
            previous.wait_recv()
            self.T[index, rows] += self.R[slot, s - 1, rows]
        self.copies[d, s, half] = self.net.send(
            self.T.at[index, rows], self.R.at[slot, s, rows], self.me.up(d)
        )

    def long(self, s):
        self.send(1, s, 0)
        self.send(-1, s, 1)

    def short(self, s):
        self.send(1, s, 1)
        self.send(-1, s, 0)

    def finish(self, half):
        for d in (1, -1):
            self.copies[d, 3, half].wait_recv()
        rows = self.slice(half)
        return self.R[0, 3, rows].astype(F32) + self.R[1, 3, rows].astype(F32)


def exchange(net, me, B1, B2, merge1, merge2):
    copies = []
    for dy in range(4):
        for dc in range(2):
            if dy + dc > 0:
                copies.append(net.send(B1.at[0], B1.at[2 * dy + dc], me.at(0, dy, dc)))

    def middle():
        for copy in copies:
            copy.wait_recv()
        B2[0] = merge1(B1)
        return [net.send(B2.at[0], B2.at[dx], me.at(dx, 0, 0)) for dx in range(1, 4)]

    def last(second):
        for copy in second:
            copy.wait_recv()
        return merge2(B2)

    return middle, last


def merge_moments(rows):
    def merge(B):
        count = B.shape[0]
        result = []
        for view in range(2):
            means = [B[k, 2 * view : 2 * view + 1] for k in range(count)]
            squares = [B[k, 2 * view + 1 : 2 * view + 2] for k in range(count)]
            mean = sum(means) / count
            square = sum(squares) + rows * sum((m - mean) * (m - mean) for m in means)
            result += [mean, square]
        return jnp.concatenate(result, axis=0)

    return merge


def merge_sums(B):
    return sum(B[k] for k in range(B.shape[0]))


def project_kernel(hf, hs, w, W, normed, spread, acc, B1, B2, ssem, rsem):
    me = Place()
    barrier(me.plane_peers())
    net = Net(ssem, rsem)
    W[me.block(0, 0)] = w[...]
    gather_plane(net, me, W)
    acc[...] = jnp.zeros_like(acc)

    def body(k, _):
        cols = pl.ds(pl.multiple_of(k * 512, 512), 512)
        piece = W[pl.ds(4 * k, 4)].reshape(512, COLS)
        acc[0] += jnp.dot(hf[:, cols], piece, preferred_element_type=F32)
        acc[1] += jnp.dot(hs[:, cols], piece, preferred_element_type=F32)
        return 0

    lax.fori_loop(0, 8, body, 0)
    for view in range(2):
        mean = jnp.sum(acc[view], axis=0, keepdims=True) / ROWS
        shifted = acc[view] - mean
        B1[0, 2 * view : 2 * view + 1] = mean
        B1[0, 2 * view + 1 : 2 * view + 2] = jnp.sum(shifted * shifted, axis=0, keepdims=True)
    middle, last = exchange(net, me, B1, B2, merge_moments(ROWS), merge_moments(8 * ROWS))
    moments = last(middle())
    for view in range(2):
        mean = moments[2 * view : 2 * view + 1]
        deviation = jnp.sqrt(moments[2 * view + 1 : 2 * view + 2] / TOKENS + epsilon)
        spread[view : view + 1] = deviation
        normed[view] = ((acc[view] - mean) / deviation).astype(BF)
    net.drain()


def pair_send(net, me, Pb, S, b):
    where = (lax.div(b, 2), pl.ds(2 * lax.rem(b, 2), 2))
    return net.send(Pb.at[where + (1 - me.c,)], S.at[where], me.sib())


def pair_add(me, Pb, S, b):
    where = (lax.div(b, 2), pl.ds(2 * lax.rem(b, 2), 2))
    S[where] += Pb[where + (me.c,)]


def store_block(Pb, b, value):
    Pb[lax.div(b, 2), pl.ds(2 * lax.rem(b, 2), 2)] = value.astype(BF).reshape(2, 2, 128, COLS)


def corr_kernel(normed, A, N, G, D, Pb, S, M1, F1, Q, M2, F2, B1, B2, E, ssem, rsem):
    me = Place()
    barrier(me.plane_peers() + me.z_peers())
    net = Net(ssem, rsem)
    A[me.z, 0:ROWS] = normed[1]
    N[0:ROWS] = normed[0]
    passed = {}

    def pass_on(s):
        for half in (0, 1):
            for d in (1, -1):
                if s < 3 or half == (0 if d == 1 else 1):
                    ref = A.at[me.Z(-d * s), pl.ds(96 * half, 96)]
                    passed[s, d, half] = net.send(ref, ref, me.up(d))

    pairs = []

    def correlate(b):
        store_block(Pb, b, dot(A[b, 0:ROWS], N[0:ROWS], ((0,), (0,))))
        pairs.append((pair_send(net, me, Pb, S, b), b))

    pass_on(0)
    n1, n2 = normed[0].astype(F32), normed[1].astype(F32)
    B1[0, 0:1] = jnp.sum(n1, axis=0, keepdims=True)
    B1[0, 1:2] = jnp.sum(n2, axis=0, keepdims=True)
    B1[0, 2:3] = jnp.sum(n1 * n2, axis=0, keepdims=True)
    B1[0, 3:4] = jnp.zeros((1, COLS), F32)
    middle, last = exchange(net, me, B1, B2, merge_sums, merge_sums)
    correlate(me.z)
    for s in range(3):
        for half in (0, 1):
            for d in (1, -1):
                passed[s, d, half].wait_recv()
        pass_on(s + 1)
        for d in (1, -1):
            correlate(me.Z(-d * (s + 1)))
        if s == 0:
            columns = middle()
        if s == 1:
            sums = last(columns) / TOKENS
            D[...] = sums[2:3]
            E[0, 0:1] = sums[1:2]
            spread_out = [net.send(E.at[0], E.at[d], me.up(d)) for d in range(1, NZ)]
    passed[3, 1, 0].wait_recv()
    passed[3, -1, 1].wait_recv()
    correlate(me.Z(4))
    for copy, b in pairs:
        copy.wait_recv()
        pair_add(me, Pb, S, b)
    halves = scatter_plane(net, me, S, M1, F1, Q, M2, F2)
    own = me.block(0, 0)
    shape = (64, COLS)
    for o in (0, 1):
        crossed = halves[o] / TOKENS
        row = own * 128 + 64 * o + lax.broadcasted_iota(jnp.int32, shape, 0)
        column = me.z * COLS + lax.broadcasted_iota(jnp.int32, shape, 1)
        G[own, 64 * o : 64 * o + 64] = jnp.where(
            row == column, 2.0 * (D[...] - 1.0), 2.0 * offdiag_weight * crossed
        ).astype(BF)
    gather_plane(net, me, G)
    for copy in spread_out:
        copy.wait_recv()

    def means(value):
        high = value.astype(BF)
        low = (value - high.astype(F32)).astype(BF)
        rest = jnp.zeros((PAD - ROWS - 2, COLS), BF)
        return jnp.concatenate([high, low, rest], axis=0)

    N[ROWS:PAD] = means(sums[0:1])
    for d in range(NZ):
        A[me.Z(-d), ROWS:PAD] = means(E[d, 0:1])
    net.drain()


def upstream_kernel(A, N, G, D, normed, spread, down, T, R, U, V, Lo, Li, ssem, rsem):
    me = Place()
    barrier(me.z_peers())
    net = Net(ssem, rsem)
    ring = ScatterZ(net, me, T, R, ROWS)
    ones = jnp.ones((16, COLS), BF)
    diagonal = (D[...] - 1.0) * 2.0
    diagonal = diagonal.astype(BF).astype(F32) * D[...]
    levels = []

    def block(d):
        b = me.Z(d)
        g = G[pl.ds(4 * b, 4)].reshape(COLS, COLS)
        t = dot(N[...], g, ((1,), (1,)))
        squares = g * g
        if d == 0:
            shape = (COLS, COLS)
            same = lax.broadcasted_iota(jnp.int32, shape, 0) == lax.broadcasted_iota(
                jnp.int32, shape, 1
            )
            squares = jnp.where(same, 0.0, squares.astype(F32)).astype(BF)
            V[...] = t[0:ROWS]
        else:
            T[b] = t[0:ROWS].astype(BF)
        slope = dot(ones, squares, ((1,), (1,)))[0:1] * (0.5 / offdiag_weight)
        if d == 0:
            slope = slope + diagonal
        out = Li if d == 0 else Lo
        out[d, 0:1] = t[ROWS : ROWS + 1] + t[ROWS + 1 : ROWS + 2]
        out[d, 1:2] = slope
        if d != 0:
            levels.append(net.send(Lo.at[d], Li.at[d], me.up(d)))
        return g, b, squares

    def first_view(g, b, squares, start):
        u = dot(A[b], g, ((1,), (0,)))
        s = dot(ones, squares, ((1,), (0,)))[0:8]
        if start:
            U[0:PAD] = u
            U[PAD : PAD + 8] = s
        else:
            U[0:PAD] += u
            U[PAD : PAD + 8] += s

    four = block(4)
    ring.long(0)
    three = block(3), block(5)
    ring.short(1)
    first_view(*four, True)
    first_view(*three[0], False)
    first_view(*three[1], False)
    two = block(2), block(6)
    ring.long(1)
    ring.short(2)
    first_view(*two[0], False)
    first_view(*two[1], False)
    one = block(1), block(7)
    ring.long(2)
    ring.short(3)
    first_view(*one[0], False)
    first_view(*one[1], False)
    first_view(*block(0), False)
    ring.long(3)

    def finish(view, upstream, level, slope):
        n = normed[view].astype(F32)
        down[view] = ((upstream - level - n * slope) / spread[view : view + 1]).astype(BF)

    level = U[ROWS : ROWS + 1] + U[ROWS + 1 : ROWS + 2]
    slope = U[PAD : PAD + 1] * (0.5 / offdiag_weight) + diagonal
    finish(0, U[0:ROWS], level, slope)
    for copy in levels:
        copy.wait_recv()
    both = merge_sums(Li)
    second = jnp.concatenate([ring.finish(0), ring.finish(1)], axis=0) + V[...]
    finish(1, second, both[0:1], both[1:2])
    net.drain()


def grads_kernel(
    down, W, hf, hs, gw, gh, T, R, V, Pb, S, M1, F1, Q, M2, F2, ssem, rsem
):
    me = Place()
    barrier(me.plane_peers() + me.z_peers())
    net = Net(ssem, rsem)
    ring = ScatterZ(net, me, T, R, 2 * ROWS)
    both = down[...].reshape(2 * ROWS, COLS)

    def block(d):
        b = me.Z(d)
        w = W[pl.ds(4 * b, 4)].reshape(COLS, COLS)
        t = dot(down[...].reshape(2 * ROWS, COLS), w, ((1,), (1,)))
        if d == 0:
            V[...] = t
        else:
            T[b] = t.astype(BF)

    pairs = []

    def weight(b):
        cols = pl.ds(pl.multiple_of(b * COLS, COLS), COLS)
        t = dot(hf[:, cols], down[0], ((0,), (0,))) + dot(hs[:, cols], down[1], ((0,), (0,)))
        store_block(Pb, b, t)
        pairs.append((pair_send(net, me, Pb, S, b), b))

    block(4)
    ring.long(0)
    block(3)
    block(5)
    ring.short(1)
    for b in range(8):
        weight(jnp.int32(b))
    block(2)
    block(6)
    ring.long(1)
    block(1)
    block(7)
    block(0)
    for copy, b in pairs:
        copy.wait_recv()
        pair_add(me, Pb, S, b)
    ring.short(2)
    halves = scatter_plane(net, me, S, M1, F1, Q, M2, F2)
    for o in (0, 1):
        gw[64 * o : 64 * o + 64] = (halves[o] / math.sqrt(TOKENS)).astype(BF)
    ring.long(2)
    ring.short(3)
    ring.long(3)
    for half in (0, 1):
        rows = pl.ds(ROWS * half, ROWS)
        gh[half] = (ring.finish(half) + V[rows]).astype(BF)
    net.drain()


VM = pl.BlockSpec(memory_space=pltpu.VMEM)


def call(kernel, ident, outs, scratch, count, args):
    return pl.pallas_call(
        kernel,
        out_shape=[jax.ShapeDtypeStruct(s, t) for s, t in outs],
        in_specs=[VM] * len(args),
        out_specs=[VM] * len(outs),
        scratch_shapes=scratch
        + [pltpu.SemaphoreType.DMA((count,)), pltpu.SemaphoreType.DMA((count,))],
        compiler_params=pltpu.CompilerParams(
            collective_id=ident, has_side_effects=True, vmem_limit_bytes=56 * 1024 * 1024
        ),
    )(*args)


def local(hidden_first, hidden_second, weight):
    W, normed, spread = call(
        project_kernel,
        1,
        [((32, 128, COLS), BF), ((2, ROWS, COLS), BF), ((2, COLS), F32)],
        [
            pltpu.VMEM((2, ROWS, COLS), F32),
            pltpu.VMEM((8, 4, COLS), F32),
            pltpu.VMEM((4, 4, COLS), F32),
        ],
        96,
        (hidden_first, hidden_second, weight),
    )
    A, N, G, D = call(
        corr_kernel,
        2,
        [
            ((NZ, PAD, COLS), BF),
            ((PAD, COLS), BF),
            ((32, 128, COLS), BF),
            ((1, COLS), F32),
        ],
        [pltpu.VMEM((4, 4, 2, 128, COLS), BF), pltpu.VMEM((4, 4, 128, COLS), BF)]
        + scatter_plane_scratch()
        + [
            pltpu.VMEM((8, 4, COLS), F32),
            pltpu.VMEM((4, 4, COLS), F32),
            pltpu.VMEM((NZ, 1, COLS), F32),
        ],
        160,
        (normed,),
    )
    (down,) = call(
        upstream_kernel,
        3,
        [((2, ROWS, COLS), BF)],
        [
            pltpu.VMEM((NZ, ROWS, COLS), BF),
            pltpu.VMEM((2, 4, ROWS, COLS), BF),
            pltpu.VMEM((PAD + 8, COLS), F32),
            pltpu.VMEM((ROWS, COLS), F32),
            pltpu.VMEM((NZ, 2, COLS), F32),
            pltpu.VMEM((NZ, 2, COLS), F32),
        ],
        32,
        (A, N, G, D, normed, spread),
    )
    gw, gh = call(
        grads_kernel,
        4,
        [((128, COLS), BF), ((2, ROWS, COLS), BF)],
        [
            pltpu.VMEM((NZ, 2 * ROWS, COLS), BF),
            pltpu.VMEM((2, 4, 2 * ROWS, COLS), BF),
            pltpu.VMEM((2 * ROWS, COLS), F32),
            pltpu.VMEM((4, 4, 2, 128, COLS), BF),
            pltpu.VMEM((4, 4, 128, COLS), BF),
        ]
        + scatter_plane_scratch(),
        64,
        (down, W, hidden_first, hidden_second),
    )
    return gw, gh[0], gh[1]


def solution(mesh):
    in_specs = (P("dp", None), P("dp", None), P("dp", "mp"))
    out_specs = (P("dp", "mp"), P("dp", "mp"), P("dp", "mp"))
    return jax.shard_map(local, mesh=mesh, in_specs=in_specs, out_specs=out_specs, check_vma=False)
```

time: 647 us -> 186 us (0.29)
  waiting for transfers between devices: 423 us -> 0 us
  Pallas kernels: 0 us -> 182 us
  blocking collectives: 164 us -> 0 us
  matrix products: 28.3 us -> 0 us
  between operations: 14.2 us -> 0.66 us
  local copies, waits for them, and re-layouts: 12.1 us -> 3.36 us
    pallas_call x0 -> x4, Pallas kernels: none -> 182 us  [call(): pl.pallas_call(kernel, out_shape=[jax.ShapeDtypeStruct(s, t) for s, t in...]
    reduce_scatter x3 -> x0, waiting for transfers between devices: 172 us -> none  [the longest x1 88 us: local(): lax.psum_scatter(contract_lead(block, norm_first).astype(jnp.bfloat16), '...]
    psum x3 -> x0, blocking collectives: 164 us -> none  [the longest x1 56.1 us: local(): variance = lax.psum(jnp.sum(shifted * shifted, axis=1), 'dp') / total_rows]
    all_gather x3 -> x0, waiting for transfers between devices: 163 us -> none  [the longest x1 56.3 us: local(): full_weight = lax.all_gather(weight, 'dp', axis=0, tiled=True)]
    unnamed x8 -> x0, waiting for transfers between devices: 87.7 us -> none
    dot_general x8 -> x0, matrix products: 28.3 us -> none  [the longest x2 10.6 us: contract_tail(): lax.dot_general(left, right, (((1,), (1,)), ((), ())), preferred_element_...]
    unnamed x11 -> x1, local copies, waits for them, and re-layouts: 9.59 us -> 1.57 us
  transfers between devices with their start and end apart: 7 -> 0, of which waited for: 7 -> 0; matrix products, arithmetic and copies ran while one was open for 2% -> 0% of each run, Pallas kernels for 0% -> 0%
where the time goes in v1:
time: 186 us
  Pallas kernels  182 us (98%)
  local copies, waits for them, and re-layouts  3.36 us (2%)
    pallas_call x4, Pallas kernels, call(): pl.pallas_call(kernel, out_shape=[jax.ShapeDtypeStruct(s, t) for s, t in...  182 us

profile of v1, /device:TPU:6, one launch (start us, length us, event | category | flops | bytes accessed | tf_op | source)
XLA Modules:
  0.0 185.8 jit_solution(4936362204386661420)
XLA Ops:
  0.6 35.8 %shard_map.58 = (bf16[32,128,512]{2,1,0:T(8,128)(2,1)}, bf16[2,192,512]{2,1,0:T(8,128)(2,1)}, f32[2,512]{1,0:T(2,128)}) custom-call(bf16[192,4096]{1,0:T(8,128)(2,1)} %hf.3, bf16[192,4096]{1,0:T(8,128)(2,1)} %hs.3, bf16[128,512]{1,0:T(8,128)(2,1)} %w.1), custom_call_target="tpu_custom_call" | custom-call | tf_op jit(solution)/shard_map/pallas_call | solution.py:575
  36.4 71.2 %shard_map.59 = (bf16[8,208,512]{2,1,0:T(8,128)(2,1)}, bf16[208,512]{1,0:T(8,128)(2,1)}, bf16[32,128,512]{2,1,0:T(8,128)(2,1)}, f32[1,512]{1,0:T(1,128)}) custom-call(bf16[2,192,512]{2,1,0:T(8,128)(2,1)} %get-tuple-element.12.normed), custom_call_target="tpu_custom_call" | custom-call | tf_op jit(solution)/shard_map/pallas_call | solution.py:575
  107.7 26.1 %shard_map.60.down = bf16[2,192,512]{2,1,0:T(8,128)(2,1)} custom-call(bf16[8,208,512]{2,1,0:T(8,128)(2,1)} %get-tuple-element.13.A, bf16[208,512]{1,0:T(8,128)(2,1)} %get-tuple-element.14.N, bf16[32,128,512]{2,1,0:T(8,128)(2,1)} %get-tuple-element.15.G, f32[1,512]{1,0:T(1,128)} %get-tuple-element.16.D, bf16[2,192,512]{2,1,0:T(8,128)(2,1)} %get-tuple-element.12.normed, ...), custom_call_target="tpu_custom_call" | custom-call | tf_op jit(solution)/shard_map/pallas_call | solution.py:575
  133.8 48.6 %shard_map.61 = (bf16[128,512]{1,0:T(8,128)(2,1)}, bf16[2,192,512]{2,1,0:T(8,128)(2,1)}) custom-call(bf16[2,192,512]{2,1,0:T(8,128)(2,1)} %shard_map.60.down, bf16[32,128,512]{2,1,0:T(8,128)(2,1)} %get-tuple-element.18.W, bf16[192,4096]{1,0:T(8,128)(2,1)} %hf.3, bf16[192,4096]{1,0:T(8,128)(2,1)} %hs.3), custom_call_target="tpu_custom_call" | custom-call | tf_op jit(solution)/shard_map/pallas_call | solution.py:575
  182.4 1.8 slice_bitcast_fusion
  184.2 1.6 copy.7

commit v2 on v0

v2 whole, which is shorter than its diff:
```python
import math

import jax
import jax.numpy as jnp
from jax import lax
from jax.experimental import pallas as pl
from jax.experimental.pallas import tpu as pltpu
from jax.sharding import PartitionSpec as P

MESH = pl.DeviceIdType.MESH
BF = jnp.bfloat16
F32 = jnp.float32

epsilon = 1e-05
offdiag_weight = 0.0051

TOKENS = 6144
ROWS = 192
PAD = 208
COLS = 512
NZ = 8
SLOTS = (0, 1, -1, 2, -2, 3, -3, 4)


def wrap(value, size):
    return lax.rem(value + size, size)


class Place:
    def __init__(self):
        dp = lax.axis_index("dp")
        self.dp = dp
        self.x = lax.div(dp, 8)
        self.y = lax.rem(lax.div(dp, 2), 4)
        self.c = lax.rem(dp, 2)
        self.z = lax.axis_index("mp")

    def X(self, d):
        return wrap(self.x + d, 4)

    def Y(self, d):
        return wrap(self.y + d, 4)

    def Z(self, d):
        return wrap(self.z + d, NZ)

    def block(self, dx, dy, dc=0):
        return self.X(dx) * 8 + self.Y(dy) * 2 + wrap(self.c + dc, 2)

    def at(self, dx, dy, dc=0):
        return {"dp": self.block(dx, dy, dc)}

    def sib(self):
        return {"dp": self.dp + 1 - 2 * self.c}

    def up(self, d):
        return {"mp": self.Z(d)}

    def plane_peers(self):
        row = [(0, dy, dc) for dy in range(4) for dc in range(2)][1:]
        column = [(dx, 0, 0) for dx in range(1, 4)]
        return [self.at(*p) for p in row + column]

    def z_peers(self):
        return [self.up(d) for d in range(1, NZ)]


class Net:
    def __init__(self, sends, recvs):
        self.sends, self.recvs = sends, recvs
        self.copies = []

    def send(self, src, dst, to):
        index = len(self.copies)
        copy = pltpu.make_async_remote_copy(
            src_ref=src,
            dst_ref=dst,
            send_sem=self.sends.at[index],
            recv_sem=self.recvs.at[index],
            device_id=to,
            device_id_type=MESH,
        )
        copy.start()
        self.copies.append(copy)
        return copy

    def drain(self):
        for copy in self.copies:
            copy.wait_send()


def barrier(peers):
    sem = pltpu.get_barrier_semaphore()
    for peer in peers:
        pl.semaphore_signal(sem, inc=1, device_id=peer, device_id_type=MESH)
    pl.semaphore_wait(sem, len(peers))


def dot(a, b, dims):
    return lax.dot_general(a, b, ((dims[0], dims[1]), ((), ())), preferred_element_type=F32)


def turn(o, first, second):
    return (first, second) if o == 0 else (second, first)


def finish(steps):
    for _ in steps:
        pass


def gather_plane(net, me, W):
    rows = W.shape[1]
    part, quarter = rows // 2, rows // 4

    def block(o, a, b):
        return me.block(*turn(o, a, b))

    def to(o, a, b):
        return me.at(*turn(o, a, b))

    def push(index, start, size, target):
        ref = W.at[index, pl.ds(start, size)]
        return net.send(ref, ref, target)

    own = me.block(0, 0)
    both = [(o, d) for d in (1, -1) for o in (0, 1)]
    first, second, far, sibs = {}, {}, {}, []

    def over(o, a):
        for d in (1, -1):
            second[o, a, d] = push(block(o, a, 0), part * o, part, to(o, 0, d))

    def share(o, a, b):
        sibs.append(push(block(o, a, b), part * o, part, me.sib()))

    for d in (1, -1, 2):
        for o in (0, 1):
            first[o, d] = push(own, part * o, part, to(o, d, 0))
    for o in (0, 1):
        over(o, 0)
    sibs.append(net.send(W.at[own], W.at[own], me.sib()))
    yield
    for d in (1, -1, 2):
        for o in (0, 1):
            first[o, d].wait_recv()
            over(o, -d)
        for o in (0, 1):
            share(o, -d, 0)
    yield
    for a in (0, -1, 1, -2):
        for o, d in both:
            second[o, a, d].wait_recv()
            far[o, a, d] = push(
                block(o, a, -d), part * o + (0 if d == 1 else quarter), quarter, to(o, 0, d)
            )
        for o, d in both:
            share(o, a, -d)
    yield
    for a in (0, -1, 1, -2):
        for o in (0, 1):
            far[o, a, 1].wait_recv()
            far[o, a, -1].wait_recv()
            share(o, a, 2)
    yield
    for copy in sibs:
        copy.wait_recv()


def scatter_plane(net, me, S, M1, F1, Q, F2, result):
    half_rows = S.shape[2] // 2

    def index(o, d):
        return me.X(d) if o == 0 else me.Y(d)

    def other(o, d):
        return me.Y(d) if o == 0 else me.X(d)

    def part(o, d, start, size=2):
        rows = pl.ds(half_rows * o, half_rows)
        if o == 0:
            return (index(o, d), pl.ds(start, size), rows)
        return (pl.ds(start, size), index(o, d), rows)

    def to(o, a, b):
        return me.at(*turn(o, a, b))

    both = [(o, d) for d in (1, -1) for o in (0, 1)]
    slot = {1: 0, -1: 1, 2: 2}
    mid, early, late, last = {}, {}, {}, {}
    for o, d in both:
        h = 0 if d == 1 else 2
        mid[o, d] = net.send(S.at[part(o, 2, h)], M1.at[o, slot[d]], to(o, d, 0))
    for o, d in both:
        h = 0 if d == 1 else 2
        early[o, d] = net.send(
            S.at[part(o, d, 2 - h)], F1.at[o, slot[d], pl.ds(2 - h, 2)], to(o, d, 0)
        )
    yield
    for o, d in both:
        h = 0 if d == 1 else 2
        mid[o, d].wait_recv()
        S[part(o, d, h)] += M1[o, slot[d]]
        late[o, d] = net.send(S.at[part(o, d, h)], F1.at[o, slot[d], pl.ds(h, 2)], to(o, d, 0))
    yield
    for o in (0, 1):
        for d in (1, -1):
            early[o, d].wait_recv()
            late[o, d].wait_recv()
        total = S[part(o, 0, 0, 4)].astype(F32) + F1[o, 0].astype(F32) + F1[o, 1].astype(F32)
        Q[o] = total.astype(BF)
        for d in (1, -1, 2):
            last[o, d] = net.send(Q.at[o, other(o, d)], F2.at[o, slot[d]], to(o, 0, d))
    yield
    for o in (0, 1):
        for d in (1, -1, 2):
            last[o, d].wait_recv()
        result.append(
            (Q[o, other(o, 0)].astype(F32) + F2[o, 0].astype(F32))
            + (F2[o, 1].astype(F32) + F2[o, 2].astype(F32))
        )


def scatter_plane_scratch(rows):
    return [
        pltpu.VMEM((4, 4, 2, rows, COLS), BF),
        pltpu.VMEM((4, 4, rows, COLS), BF),
        pltpu.VMEM((2, 2, 2, rows // 2, COLS), BF),
        pltpu.VMEM((2, 2, 4, rows // 2, COLS), BF),
        pltpu.VMEM((2, 4, rows // 2, COLS), BF),
        pltpu.VMEM((2, 3, rows // 2, COLS), BF),
    ]


class ScatterZ:
    def __init__(self, net, me, T, R, rows):
        self.net, self.me, self.T, self.R = net, me, T, R
        self.half = rows // 2
        self.copies = {}

    def slice(self, half):
        return pl.ds(half * self.half, self.half)

    def send(self, d, s, half):
        slot = 0 if d == 1 else 1
        index = self.me.Z(d * (4 - s))
        rows = self.slice(half)
        previous = self.copies.get((d, s - 1, half))
        if previous is not None:
            previous.wait_recv()
            self.T[index, rows] += self.R[slot, s - 1, rows]
        self.copies[d, s, half] = self.net.send(
            self.T.at[index, rows], self.R.at[slot, s, rows], self.me.up(d)
        )

    def long(self, s):
        self.send(1, s, 0)
        self.send(-1, s, 1)

    def short(self, s):
        self.send(1, s, 1)
        self.send(-1, s, 0)

    def finish(self, half):
        for d in (1, -1):
            self.copies[d, 3, half].wait_recv()
        rows = self.slice(half)
        return self.R[0, 3, rows].astype(F32) + self.R[1, 3, rows].astype(F32)


def exchange(net, me, B1, B2, merge1, merge2):
    copies = []
    for dy in range(4):
        for dc in range(2):
            if dy + dc > 0:
                copies.append(net.send(B1.at[0], B1.at[2 * dy + dc], me.at(0, dy, dc)))

    def middle():
        for copy in copies:
            copy.wait_recv()
        B2[0] = merge1(B1)
        return [net.send(B2.at[0], B2.at[dx], me.at(dx, 0, 0)) for dx in range(1, 4)]

    def last(second):
        for copy in second:
            copy.wait_recv()
        return merge2(B2)

    return middle, last


def merge_moments(rows):
    def merge(B):
        count = B.shape[0]
        result = []
        for view in range(2):
            means = [B[k, 2 * view : 2 * view + 1] for k in range(count)]
            squares = [B[k, 2 * view + 1 : 2 * view + 2] for k in range(count)]
            mean = sum(means) / count
            square = sum(squares) + rows * sum((m - mean) * (m - mean) for m in means)
            result += [mean, square]
        return jnp.concatenate(result, axis=0)

    return merge


def merge_sums(B):
    return sum(B[k] for k in range(B.shape[0]))


class Pairs:
    def __init__(self, net, me, Pb, S):
        self.net, self.me, self.Pb, self.S = net, me, Pb, S
        self.copies = []

    def put(self, slot, value):
        rows = pl.ds(16 * slot, 16)
        self.Pb[:, :, :, rows] = value.astype(BF).reshape(4, 4, 2, 16, COLS)
        copy = self.net.send(
            self.Pb.at[:, :, 1 - self.me.c, rows], self.S.at[:, :, rows], self.me.sib()
        )
        self.copies.append((copy, slot))

    def add(self):
        for copy, slot in self.copies:
            rows = pl.ds(16 * slot, 16)
            copy.wait_recv()
            self.S[:, :, rows] += self.Pb[:, :, self.me.c, rows]


class Blocks:
    def __init__(self, net, me, Pb, S):
        self.net, self.me, self.Pb, self.S = net, me, Pb, S
        self.copies = []

    def where(self, b):
        return (b // 2, pl.ds(2 * (b % 2), 2))

    def put(self, b, value):
        where = self.where(b)
        self.Pb[where] = value.astype(BF).reshape(2, 2, 128, COLS)
        copy = self.net.send(
            self.Pb.at[where + (1 - self.me.c,)], self.S.at[where], self.me.sib()
        )
        self.copies.append((copy, where))

    def add(self):
        for copy, where in self.copies:
            copy.wait_recv()
            self.S[where] += self.Pb[where + (self.me.c,)]


class GatherZ:
    def __init__(self, net, me, A):
        self.net, self.me, self.A = net, me, A
        self.copies = {}

    def send(self, s, d, half):
        ref = self.A.at[self.me.Z(-d * s), pl.ds(96 * half, 96)]
        self.copies[s, d, half] = self.net.send(ref, ref, self.me.up(d))

    def start(self):
        for turn_ in (0, 1):
            for d in (1, -1):
                self.send(0, d, turn_ if d == 1 else 1 - turn_)

    def step(self, s):
        for turn_ in (0, 1):
            for d in (1, -1):
                half = turn_ if d == 1 else 1 - turn_
                if (s, d, half) in self.copies:
                    self.copies[s, d, half].wait_recv()
                    if s < 2 or (s == 2 and turn_ == 0):
                        self.send(s + 1, d, half)


def means(value):
    high = value.astype(BF)
    low = (value - high.astype(F32)).astype(BF)
    rest = jnp.zeros((PAD - ROWS - 2, COLS), BF)
    return jnp.concatenate([high, low, rest], axis=0)


def kernel(
    hf, hs, w, gw, g1, g2,
    H, W, acc, DN, A1, A2, X1, X2, Y1, Y2, E, GA, GB, G2, U, T1, R1, T2, R2, V1, V2,
    PA, SA, MA, FA, QA, LA, PB, SB, MB, FB, QB, LB, PG, SG, MG, FG, QG, LG,
    lsem, ssem, rsem,
):
    me = Place()
    net = Net(ssem, rsem)
    own = me.block(0, 0)
    loads = [
        pltpu.make_async_copy(w, W.at[own], lsem.at[0]),
        pltpu.make_async_copy(hf, H.at[pl.ds(0, ROWS)], lsem.at[1]),
        pltpu.make_async_copy(hs, H.at[pl.ds(ROWS, ROWS)], lsem.at[2]),
    ]
    for load in loads:
        load.start()
    barrier(me.plane_peers() + me.z_peers())
    loads[0].wait()
    finish(gather_plane(net, me, W))
    loads[1].wait()
    loads[2].wait()

    acc[...] = jnp.zeros_like(acc)

    def project(k, _):
        cols = pl.ds(pl.multiple_of(k * 1024, 1024), 1024)
        piece = W[pl.ds(8 * k, 8)].reshape(1024, COLS)
        acc[...] += jnp.dot(H[:, cols], piece, preferred_element_type=F32)
        return 0

    lax.fori_loop(0, 4, project, 0)

    def view(v):
        return slice(v * ROWS, (v + 1) * ROWS)

    for v in range(2):
        mean = jnp.sum(acc[view(v)], axis=0, keepdims=True) / ROWS
        shifted = acc[view(v)] - mean
        X1[0, 2 * v : 2 * v + 1] = mean
        X1[0, 2 * v + 1 : 2 * v + 2] = jnp.sum(shifted * shifted, axis=0, keepdims=True)
    middle, last = exchange(net, me, X1, X2, merge_moments(ROWS), merge_moments(8 * ROWS))
    moments = last(middle())
    spread = []
    for v, A in ((0, A1), (1, A2)):
        mean = moments[2 * v : 2 * v + 1]
        spread.append(jnp.sqrt(moments[2 * v + 1 : 2 * v + 2] / TOKENS + epsilon))
        A[me.z, 0:ROWS] = ((acc[view(v)] - mean) / spread[v]).astype(BF)

    gz2 = GatherZ(net, me, A2)
    gz1 = GatherZ(net, me, A1)
    gz2.start()
    n1, n2 = A1[me.z, 0:ROWS].astype(F32), A2[me.z, 0:ROWS].astype(F32)
    Y1[0, 0:1] = jnp.sum(n1, axis=0, keepdims=True)
    Y1[0, 1:2] = jnp.sum(n2, axis=0, keepdims=True)
    Y1[0, 2:3] = jnp.sum(n1 * n2, axis=0, keepdims=True)
    Y1[0, 3:4] = jnp.zeros((1, COLS), F32)
    middle, last = exchange(net, me, Y1, Y2, merge_sums, merge_sums)
    groups = (Pairs(net, me, PA, SA), Pairs(net, me, PB, SB))

    def correlate(slot):
        value = dot(A2[me.Z(SLOTS[slot]), 0:ROWS], A1[me.z, 0:ROWS], ((0,), (0,)))
        groups[slot // 4].put(slot % 4, value)

    halves_a, halves_b = [], []
    scatter_a = scatter_plane(net, me, SA, MA, FA, QA, LA, halves_a)
    scatter_b = scatter_plane(net, me, SB, MB, FB, QB, LB, halves_b)
    correlate(0)
    gz2.step(0)
    correlate(1)
    correlate(2)
    columns = middle()
    gz2.step(1)
    correlate(3)
    groups[0].add()
    next(scatter_a)
    correlate(4)
    sums = last(columns) / TOKENS
    E[0, 0:2] = sums[0:2]
    tops = [net.send(E.at[0], E.at[d], me.up(d)) for d in range(1, NZ)]
    gz2.step(2)
    correlate(5)
    correlate(6)
    next(scatter_a)
    gz2.step(3)
    gz1.start()
    correlate(7)
    groups[1].add()
    next(scatter_b)
    next(scatter_a)
    next(scatter_b)

    diagonal = 2.0 * (sums[2:3] - 1.0)

    def loss_grad(G, halves, group):
        for o in (0, 1):
            rows = pl.ds(32 * o, 32)
            value = (2.0 * offdiag_weight / TOKENS) * halves[o]
            if group == 0 and o == 0:
                row = lax.broadcasted_iota(jnp.int32, (32, COLS), 0)
                column = lax.broadcasted_iota(jnp.int32, (32, COLS), 1)
                same = jnp.logical_and(row < 16, row + 16 * own == column)
                value = jnp.where(same, diagonal, value)
            G[own, rows] = value.astype(BF)

    across = []

    def turn_over(G, group):
        for k in range(4):
            slot = 4 * group + k
            offset = SLOTS[slot]
            source = G.at[own, pl.ds(16 * k, 16)]
            if offset == 0:
                G2[own, 0:16] = G[own, 0:16]
            else:
                there = 7 if offset == 4 else SLOTS.index(-offset)
                across.append(
                    net.send(source, G2.at[own, pl.ds(16 * there, 16)], me.up(offset))
                )

    finish(scatter_a)
    loss_grad(GA, halves_a, 0)
    gather_a = gather_plane(net, me, GA)
    next(gather_a)
    turn_over(GA, 0)
    next(scatter_b)
    gz1.step(0)
    next(gather_a)
    finish(scatter_b)
    loss_grad(GB, halves_b, 1)
    gather_b = gather_plane(net, me, GB)
    next(gather_b)
    turn_over(GB, 1)
    next(gather_a)
    next(gather_b)
    next(gather_a)
    gz1.step(1)
    for copy in tops:
        copy.wait_recv()
    for d in range(NZ):
        A1[me.Z(-d), ROWS:PAD] = means(E[d, 0:1])
        A2[me.Z(-d), ROWS:PAD] = means(E[d, 1:2])
    next(gather_b)
    finish(gather_a)
    ones = jnp.ones((16, COLS), BF)

    def upstream(A, G, slot, dims, start):
        rows = pl.ds(16 * (slot % (G.shape[1] // 16)), 16)
        g = G[:, rows].reshape(COLS, COLS)
        squares = g * g
        if slot == 0:
            shape = (COLS, COLS)
            same = lax.broadcasted_iota(jnp.int32, shape, 0) == lax.broadcasted_iota(
                jnp.int32, shape, 1
            )
            squares = jnp.where(same, 0.0, squares.astype(F32)).astype(BF)
        u = dot(A[me.Z(SLOTS[slot])], g, ((1,), dims))
        s = dot(ones, squares, ((1,), dims))[0:8]
        if start:
            U[0:PAD] = u
            U[PAD : PAD + 8] = s
        else:
            U[0:PAD] += u
            U[PAD : PAD + 8] += s

    own_slope = diagonal.astype(BF).astype(F32) * sums[2:3]

    def down(v, A):
        level = U[ROWS : ROWS + 1] + U[ROWS + 1 : ROWS + 2]
        slope = U[PAD : PAD + 1] * (0.5 / offdiag_weight) + own_slope
        n = A[me.z, 0:ROWS].astype(F32)
        DN[view(v)] = ((U[0:ROWS] - level - n * slope) / spread[v]).astype(BF)

    def partial(v, T, V, d):
        b = me.Z(d)
        piece = W[pl.ds(4 * b, 4)].reshape(COLS, COLS)
        t = dot(DN[view(v)], piece, ((1,), (1,)))
        if d == 0:
            V[...] = t
        else:
            T[b] = t.astype(BF)

    for slot in range(4):
        upstream(A2, GA, slot, (0,), slot == 0)
    next(gather_b)
    gz1.step(2)
    for copy in across:
        copy.wait_recv()
    gather_2 = gather_plane(net, me, G2)
    next(gather_2)
    finish(gather_b)
    for slot in range(4, 8):
        upstream(A2, GB, slot, (0,), False)
    down(0, A1)
    ring1 = ScatterZ(net, me, T1, R1, ROWS)
    ring2 = ScatterZ(net, me, T2, R2, ROWS)
    gz1.step(3)
    partial(0, T1, V1, 4)
    ring1.long(0)
    partial(0, T1, V1, 3)
    partial(0, T1, V1, -3)
    ring1.short(1)
    next(gather_2)
    partial(0, T1, V1, 2)
    partial(0, T1, V1, -2)
    ring1.long(1)
    ring1.short(2)
    partial(0, T1, V1, 1)
    partial(0, T1, V1, -1)
    next(gather_2)
    ring1.long(2)
    ring1.short(3)
    partial(0, T1, V1, 0)
    next(gather_2)
    ring1.long(3)
    finish(gather_2)
    for slot in range(8):
        upstream(A1, G2, slot, (1,), slot == 0)
    down(1, A2)
    partial(1, T2, V2, 4)
    ring2.long(0)
    partial(1, T2, V2, 3)
    partial(1, T2, V2, -3)
    ring2.short(1)
    weight = Blocks(net, me, PG, SG)
    for b in range(8):
        cols = pl.ds(b * COLS, COLS)
        weight.put(b, dot(H[:, cols], DN[...], ((0,), (0,))))
    partial(1, T2, V2, 2)
    partial(1, T2, V2, -2)
    ring2.long(1)
    partial(1, T2, V2, 1)
    partial(1, T2, V2, -1)
    ring2.short(2)
    halves_g = []
    scatter_g = scatter_plane(net, me, SG, MG, FG, QG, LG, halves_g)
    weight.add()
    next(scatter_g)
    ring2.long(2)
    next(scatter_g)
    ring2.short(3)
    partial(1, T2, V2, 0)
    next(scatter_g)
    ring2.long(3)
    for ring, V, out in ((ring1, V1, g1), (ring2, V2, g2)):
        for half in (0, 1):
            rows = pl.ds(96 * half, 96)
            out[rows] = (ring.finish(half) + V[rows]).astype(BF)
    finish(scatter_g)
    for o in (0, 1):
        gw[64 * o : 64 * o + 64] = (halves_g[o] / math.sqrt(TOKENS)).astype(BF)
    net.drain()


def local(hidden_first, hidden_second, weight):
    vm = pl.BlockSpec(memory_space=pltpu.VMEM)
    hbm = pl.BlockSpec(memory_space=pl.ANY)
    count = 640
    return pl.pallas_call(
        kernel,
        out_shape=[
            jax.ShapeDtypeStruct((128, COLS), BF),
            jax.ShapeDtypeStruct((ROWS, COLS), BF),
            jax.ShapeDtypeStruct((ROWS, COLS), BF),
        ],
        in_specs=[hbm] * 3,
        out_specs=[vm] * 3,
        scratch_shapes=[
            pltpu.VMEM((2 * ROWS, 4096), BF),
            pltpu.VMEM((32, 128, COLS), BF),
            pltpu.VMEM((2 * ROWS, COLS), F32),
            pltpu.VMEM((2 * ROWS, COLS), BF),
            pltpu.VMEM((NZ, PAD, COLS), BF),
            pltpu.VMEM((NZ, PAD, COLS), BF),
            pltpu.VMEM((8, 4, COLS), F32),
            pltpu.VMEM((4, 4, COLS), F32),
            pltpu.VMEM((8, 4, COLS), F32),
            pltpu.VMEM((4, 4, COLS), F32),
            pltpu.VMEM((NZ, 2, COLS), F32),
            pltpu.VMEM((32, 64, COLS), BF),
            pltpu.VMEM((32, 64, COLS), BF),
            pltpu.VMEM((32, 128, COLS), BF),
            pltpu.VMEM((PAD + 8, COLS), F32),
            pltpu.VMEM((NZ, ROWS, COLS), BF),
            pltpu.VMEM((2, 4, ROWS, COLS), BF),
            pltpu.VMEM((NZ, ROWS, COLS), BF),
            pltpu.VMEM((2, 4, ROWS, COLS), BF),
            pltpu.VMEM((ROWS, COLS), F32),
            pltpu.VMEM((ROWS, COLS), F32),
        ]
        + scatter_plane_scratch(64)
        + scatter_plane_scratch(64)
        + scatter_plane_scratch(128)
        + [
            pltpu.SemaphoreType.DMA((3,)),
            pltpu.SemaphoreType.DMA((count,)),
            pltpu.SemaphoreType.DMA((count,)),
        ],
        compiler_params=pltpu.CompilerParams(
            collective_id=1, has_side_effects=True, vmem_limit_bytes=60 * 1024 * 1024
        ),
    )(hidden_first, hidden_second, weight)


def solution(mesh):
    in_specs = (P("dp", None), P("dp", None), P("dp", "mp"))
    out_specs = (P("dp", "mp"), P("dp", "mp"), P("dp", "mp"))
    return jax.shard_map(local, mesh=mesh, in_specs=in_specs, out_specs=out_specs, check_vma=False)
```

time: 647 us -> 144 us (0.22)
  waiting for transfers between devices: 423 us -> 0 us
  blocking collectives: 164 us -> 0 us
  Pallas kernels: 0 us -> 138 us
  matrix products: 28.3 us -> 0 us
  between operations: 14.2 us -> 0.64 us
  local copies, waits for them, and re-layouts: 12.1 us -> 4.8 us
    reduce_scatter x3 -> x0, waiting for transfers between devices: 172 us -> none  [the longest x1 88 us: local(): lax.psum_scatter(contract_lead(block, norm_first).astype(jnp.bfloat16), '...]
    psum x3 -> x0, blocking collectives: 164 us -> none  [the longest x1 56.1 us: local(): variance = lax.psum(jnp.sum(shifted * shifted, axis=1), 'dp') / total_rows]
    all_gather x3 -> x0, waiting for transfers between devices: 163 us -> none  [the longest x1 56.3 us: local(): full_weight = lax.all_gather(weight, 'dp', axis=0, tiled=True)]
    pallas_call x0 -> x1, Pallas kernels: none -> 138 us  [local(): pl.pallas_call(kernel, out_shape=[jax.ShapeDtypeStruct((128, COLS), BF),...]
    unnamed x8 -> x0, waiting for transfers between devices: 87.7 us -> none
    dot_general x8 -> x0, matrix products: 28.3 us -> none  [the longest x2 10.6 us: contract_tail(): lax.dot_general(left, right, (((1,), (1,)), ((), ())), preferred_element_...]
  transfers between devices with their start and end apart: 7 -> 0, of which waited for: 7 -> 0; matrix products, arithmetic and copies ran while one was open for 2% -> 0% of each run, Pallas kernels for 0% -> 0%
where the time goes in v2:
time: 144 us; the launch traced here: 143 us
  Pallas kernels  138 us (96%)
  local copies, waits for them, and re-layouts  4.8 us (3%)
    pallas_call x1, Pallas kernels, local(): pl.pallas_call(kernel, out_shape=[jax.ShapeDtypeStruct((128, COLS), BF),...  138 us
    unnamed x3, local copies, waits for them, and re-layouts  4.8 us

profile of v2, /device:TPU:6, one launch (start us, length us, event | category | flops | bytes accessed | tf_op | source)
XLA Modules:
  0.0 143.4 jit_solution(12632491779666102817)
XLA Ops:
  0.6 137.9 %shard_map.58 = (bf16[128,512]{1,0:T(8,128)(2,1)}, bf16[192,512]{1,0:T(8,128)(2,1)}, bf16[192,512]{1,0:T(8,128)(2,1)}) custom-call(bf16[192,4096]{1,0:T(8,128)(2,1)} %hf.1, bf16[192,4096]{1,0:T(8,128)(2,1)} %hs.1, bf16[128,512]{1,0:T(8,128)(2,1)} %w.1), custom_call_target="tpu_custom_call" | custom-call | tf_op jit(solution)/shard_map/pallas_call | solution.py:641
  138.6 1.6 %copy.9 = bf16[128,512]{1,0:T(8,128)(2,1)} copy(bf16[128,512]{1,0:T(8,128)(2,1)} %get-tuple-element.6) | data formatting | bytes 262144
  140.1 1.6 %copy.10 = bf16[192,512]{1,0:T(8,128)(2,1)} copy(bf16[192,512]{1,0:T(8,128)(2,1)} %get-tuple-element.7) | data formatting | bytes 393216
  141.8 1.6 %copy.11 = bf16[192,512]{1,0:T(8,128)(2,1)} copy(bf16[192,512]{1,0:T(8,128)(2,1)} %get-tuple-element.8) | data formatting | bytes 393216

commit v3 on v2

--- a/solution.py
+++ b/solution.py
@@ -47,6 +47,9 @@
     def block(self, dx, dy, dc=0):
         return self.X(dx) * 8 + self.Y(dy) * 2 + wrap(self.c + dc, 2)
 
+    def chip(self, dx, dy):
+        return self.X(dx) * 4 + self.Y(dy)
+
     def at(self, dx, dy, dc=0):
         return {"dp": self.block(dx, dy, dc)}
 
@@ -66,27 +69,40 @@
 
 
 class Net:
-    def __init__(self, sends, recvs):
-        self.sends, self.recvs = sends, recvs
-        self.copies = []
-
-    def send(self, src, dst, to):
-        index = len(self.copies)
-        copy = pltpu.make_async_remote_copy(
+    def __init__(self, me, sent, recvs):
+        self.me, self.sent, self.recvs = me, sent, recvs
+        self.count = 0
+        self.totals = []
+
+    def group(self):
+        self.count += 1
+        return self.count - 1
+
+    def sender(self, total):
+        self.totals.append(total)
+        return len(self.totals) - 1
+
+    def copy(self, src, dst, to, sender, group):
+        return pltpu.make_async_remote_copy(
             src_ref=src,
             dst_ref=dst,
-            send_sem=self.sends.at[index],
-            recv_sem=self.recvs.at[index],
+            send_sem=self.sent.at[sender],
+            recv_sem=self.recvs.at[group],
             device_id=to,
             device_id_type=MESH,
         )
+
+    def send(self, src, dst, to, sender, group=None):
+        copy = self.copy(src, dst, to, sender, self.group() if group is None else group)
         copy.start()
-        self.copies.append(copy)
         return copy
 
+    def wait(self, group, total):
+        self.copy(total, total, self.me.sib(), 0, group).wait_recv()
+
     def drain(self):
-        for copy in self.copies:
-            copy.wait_send()
+        for sender, total in enumerate(self.totals):
+            self.copy(total, total, self.me.sib(), sender, 0).wait_send()
 
 
 def barrier(peers):
@@ -110,36 +126,39 @@
 
 
 def gather_plane(net, me, W):
-    rows = W.shape[1]
+    rows = W.shape[2]
     part, quarter = rows // 2, rows // 4
 
     def block(o, a, b):
-        return me.block(*turn(o, a, b))
+        return me.chip(*turn(o, a, b))
 
     def to(o, a, b):
         return me.at(*turn(o, a, b))
 
-    def push(index, start, size, target):
-        ref = W.at[index, pl.ds(start, size)]
-        return net.send(ref, ref, target)
-
-    own = me.block(0, 0)
+    def push(index, start, size, target, group=None):
+        ref = W.at[index, me.c, pl.ds(start, size)]
+        return net.send(ref, ref, target, many, group)
+
+    own = me.chip(0, 0)
+    block_ref = W.at[own, me.c]
     both = [(o, d) for d in (1, -1) for o in (0, 1)]
-    first, second, far, sibs = {}, {}, {}, []
+    first, second = {}, {}
+    shared, far = net.group(), [net.group() for _ in range(4)]
+    many, one = net.sender(W.at[pl.ds(0, 15)]), net.sender(block_ref)
 
     def over(o, a):
         for d in (1, -1):
             second[o, a, d] = push(block(o, a, 0), part * o, part, to(o, 0, d))
 
     def share(o, a, b):
-        sibs.append(push(block(o, a, b), part * o, part, me.sib()))
+        push(block(o, a, b), part * o, part, me.sib(), shared)
 
     for d in (1, -1, 2):
         for o in (0, 1):
             first[o, d] = push(own, part * o, part, to(o, d, 0))
     for o in (0, 1):
         over(o, 0)
-    sibs.append(net.send(W.at[own], W.at[own], me.sib()))
+    net.send(block_ref, block_ref, me.sib(), one, shared)
     yield
     for d in (1, -1, 2):
         for o in (0, 1):
@@ -148,23 +167,20 @@
         for o in (0, 1):
             share(o, -d, 0)
     yield
-    for a in (0, -1, 1, -2):
+    for k, a in enumerate((0, -1, 1, -2)):
         for o, d in both:
             second[o, a, d].wait_recv()
-            far[o, a, d] = push(
-                block(o, a, -d), part * o + (0 if d == 1 else quarter), quarter, to(o, 0, d)
-            )
+            start = part * o + (0 if d == 1 else quarter)
+            push(block(o, a, -d), start, quarter, to(o, 0, d), far[k])
         for o, d in both:
             share(o, a, -d)
     yield
-    for a in (0, -1, 1, -2):
+    for k, a in enumerate((0, -1, 1, -2)):
+        net.wait(far[k], block_ref)
         for o in (0, 1):
-            far[o, a, 1].wait_recv()
-            far[o, a, -1].wait_recv()
             share(o, a, 2)
     yield
-    for copy in sibs:
-        copy.wait_recv()
+    net.wait(shared, W.at[:, 1 - me.c])
 
 
 def scatter_plane(net, me, S, M1, F1, Q, F2, result):
@@ -187,34 +203,34 @@
 
     both = [(o, d) for d in (1, -1) for o in (0, 1)]
     slot = {1: 0, -1: 1, 2: 2}
-    mid, early, late, last = {}, {}, {}, {}
+    mid = {}
+    many, few = net.sender(S.at[pl.ds(0, 3)]), net.sender(F2)
+    parts = [net.group() for _ in (0, 1)]
+    ends = [net.group() for _ in (0, 1)]
     for o, d in both:
         h = 0 if d == 1 else 2
-        mid[o, d] = net.send(S.at[part(o, 2, h)], M1.at[o, slot[d]], to(o, d, 0))
+        mid[o, d] = net.send(S.at[part(o, 2, h)], M1.at[o, slot[d]], to(o, d, 0), many)
     for o, d in both:
         h = 0 if d == 1 else 2
-        early[o, d] = net.send(
-            S.at[part(o, d, 2 - h)], F1.at[o, slot[d], pl.ds(2 - h, 2)], to(o, d, 0)
-        )
+        there = F1.at[o, slot[d], pl.ds(2 - h, 2)]
+        net.send(S.at[part(o, d, 2 - h)], there, to(o, d, 0), many, parts[o])
     yield
     for o, d in both:
         h = 0 if d == 1 else 2
         mid[o, d].wait_recv()
         S[part(o, d, h)] += M1[o, slot[d]]
-        late[o, d] = net.send(S.at[part(o, d, h)], F1.at[o, slot[d], pl.ds(h, 2)], to(o, d, 0))
+        there = F1.at[o, slot[d], pl.ds(h, 2)]
+        net.send(S.at[part(o, d, h)], there, to(o, d, 0), many, parts[o])
     yield
     for o in (0, 1):
-        for d in (1, -1):
-            early[o, d].wait_recv()
-            late[o, d].wait_recv()
+        net.wait(parts[o], F1.at[o])
         total = S[part(o, 0, 0, 4)].astype(F32) + F1[o, 0].astype(F32) + F1[o, 1].astype(F32)
         Q[o] = total.astype(BF)
         for d in (1, -1, 2):
-            last[o, d] = net.send(Q.at[o, other(o, d)], F2.at[o, slot[d]], to(o, 0, d))
+            net.send(Q.at[o, other(o, d)], F2.at[o, slot[d]], to(o, 0, d), few, ends[o])
     yield
     for o in (0, 1):
-        for d in (1, -1, 2):
-            last[o, d].wait_recv()
+        net.wait(ends[o], F2.at[o])
         result.append(
             (Q[o, other(o, 0)].astype(F32) + F2[o, 0].astype(F32))
             + (F2[o, 1].astype(F32) + F2[o, 2].astype(F32))
@@ -233,57 +249,61 @@
 
 
 class ScatterZ:
-    def __init__(self, net, me, T, R, rows):
+    def __init__(self, net, me, T, R):
         self.net, self.me, self.T, self.R = net, me, T, R
-        self.half = rows // 2
+        self.sender = net.sender(T.at[pl.ds(0, NZ - 1)])
         self.copies = {}
 
-    def slice(self, half):
-        return pl.ds(half * self.half, self.half)
-
-    def send(self, d, s, half):
+    def send(self, d, s, piece):
         slot = 0 if d == 1 else 1
         index = self.me.Z(d * (4 - s))
-        rows = self.slice(half)
-        previous = self.copies.get((d, s - 1, half))
+        rows = pl.ds(48 * piece, 48)
+        previous = self.copies.get((d, s - 1, piece))
         if previous is not None:
             previous.wait_recv()
             self.T[index, rows] += self.R[slot, s - 1, rows]
-        self.copies[d, s, half] = self.net.send(
-            self.T.at[index, rows], self.R.at[slot, s, rows], self.me.up(d)
+        self.copies[d, s, piece] = self.net.send(
+            self.T.at[index, rows], self.R.at[slot, s, rows], self.me.up(d), self.sender
         )
 
     def long(self, s):
-        self.send(1, s, 0)
-        self.send(-1, s, 1)
+        for i in (0, 1):
+            self.send(1, s, i)
+            self.send(-1, s, 2 + i)
 
     def short(self, s):
-        self.send(1, s, 1)
-        self.send(-1, s, 0)
-
-    def finish(self, half):
-        for d in (1, -1):
-            self.copies[d, 3, half].wait_recv()
-        rows = self.slice(half)
-        return self.R[0, 3, rows].astype(F32) + self.R[1, 3, rows].astype(F32)
+        for i in (0, 1):
+            self.send(1, s, 2 + i)
+            self.send(-1, s, i)
+
+    def finish(self, V, write):
+        for piece in (2, 0, 3, 1):
+            rows = pl.ds(48 * piece, 48)
+            for d in (1, -1):
+                self.copies[d, 3, piece].wait_recv()
+            write(
+                48 * piece,
+                V[rows] + (self.R[0, 3, rows].astype(F32) + self.R[1, 3, rows].astype(F32)),
+            )
 
 
 def exchange(net, me, B1, B2, merge1, merge2):
-    copies = []
+    row, column = B1.at[pl.ds(1, 7)], B2.at[pl.ds(1, 3)]
+    one, two = net.group(), net.group()
+    by = net.sender(row), net.sender(column)
     for dy in range(4):
         for dc in range(2):
             if dy + dc > 0:
-                copies.append(net.send(B1.at[0], B1.at[2 * dy + dc], me.at(0, dy, dc)))
+                net.send(B1.at[0], B1.at[2 * dy + dc], me.at(0, dy, dc), by[0], one)
 
     def middle():
-        for copy in copies:
-            copy.wait_recv()
+        net.wait(one, row)
         B2[0] = merge1(B1)
-        return [net.send(B2.at[0], B2.at[dx], me.at(dx, 0, 0)) for dx in range(1, 4)]
-
-    def last(second):
-        for copy in second:
-            copy.wait_recv()
+        for dx in range(1, 4):
+            net.send(B2.at[0], B2.at[dx], me.at(dx, 0, 0), by[1], two)
+
+    def last():
+        net.wait(two, column)
         return merge2(B2)
 
     return middle, last
@@ -311,27 +331,29 @@
 class Pairs:
     def __init__(self, net, me, Pb, S):
         self.net, self.me, self.Pb, self.S = net, me, Pb, S
-        self.copies = []
+        self.group, self.sender = net.group(), net.sender(S)
+        self.places = []
 
     def put(self, slot, value):
         rows = pl.ds(16 * slot, 16)
         self.Pb[:, :, :, rows] = value.astype(BF).reshape(4, 4, 2, 16, COLS)
-        copy = self.net.send(
-            self.Pb.at[:, :, 1 - self.me.c, rows], self.S.at[:, :, rows], self.me.sib()
-        )
-        self.copies.append((copy, slot))
+        there = self.S.at[:, :, rows]
+        other = self.Pb.at[:, :, 1 - self.me.c, rows]
+        self.net.send(other, there, self.me.sib(), self.sender, self.group)
+        self.places.append(slot)
 
     def add(self):
-        for copy, slot in self.copies:
+        self.net.wait(self.group, self.S)
+        for slot in self.places:
             rows = pl.ds(16 * slot, 16)
-            copy.wait_recv()
             self.S[:, :, rows] += self.Pb[:, :, self.me.c, rows]
 
 
 class Blocks:
     def __init__(self, net, me, Pb, S):
         self.net, self.me, self.Pb, self.S = net, me, Pb, S
-        self.copies = []
+        self.group, self.sender = net.group(), net.sender(S)
+        self.places = []
 
     def where(self, b):
         return (b // 2, pl.ds(2 * (b % 2), 2))
@@ -339,39 +361,39 @@
     def put(self, b, value):
         where = self.where(b)
         self.Pb[where] = value.astype(BF).reshape(2, 2, 128, COLS)
-        copy = self.net.send(
-            self.Pb.at[where + (1 - self.me.c,)], self.S.at[where], self.me.sib()
-        )
-        self.copies.append((copy, where))
+        other = self.Pb.at[where + (1 - self.me.c,)]
+        self.net.send(other, self.S.at[where], self.me.sib(), self.sender, self.group)
+        self.places.append(where)
 
     def add(self):
-        for copy, where in self.copies:
-            copy.wait_recv()
+        self.net.wait(self.group, self.S)
+        for where in self.places:
             self.S[where] += self.Pb[where + (self.me.c,)]
 
 
 class GatherZ:
     def __init__(self, net, me, A):
         self.net, self.me, self.A = net, me, A
+        self.sender = net.sender(A.at[pl.ds(0, NZ - 1), pl.ds(0, ROWS)])
         self.copies = {}
 
-    def send(self, s, d, half):
-        ref = self.A.at[self.me.Z(-d * s), pl.ds(96 * half, 96)]
-        self.copies[s, d, half] = self.net.send(ref, ref, self.me.up(d))
+    def order(self):
+        return [(1, 0), (-1, 2), (1, 1), (-1, 3), (1, 2), (-1, 0), (1, 3), (-1, 1)]
+
+    def send(self, s, d, piece):
+        ref = self.A.at[self.me.Z(-d * s), pl.ds(48 * piece, 48)]
+        self.copies[s, d, piece] = self.net.send(ref, ref, self.me.up(d), self.sender)
 
     def start(self):
-        for turn_ in (0, 1):
-            for d in (1, -1):
-                self.send(0, d, turn_ if d == 1 else 1 - turn_)
+        for d, piece in self.order():
+            self.send(0, d, piece)
 
     def step(self, s):
-        for turn_ in (0, 1):
-            for d in (1, -1):
-                half = turn_ if d == 1 else 1 - turn_
-                if (s, d, half) in self.copies:
-                    self.copies[s, d, half].wait_recv()
-                    if s < 2 or (s == 2 and turn_ == 0):
-                        self.send(s + 1, d, half)
+        for place, (d, piece) in enumerate(self.order()):
+            if (s, d, piece) in self.copies:
+                self.copies[s, d, piece].wait_recv()
+                if s < 2 or (s == 2 and place < 4):
+                    self.send(s + 1, d, piece)
 
 
 def means(value):
@@ -382,16 +404,17 @@
 
 
 def kernel(
-    hf, hs, w, gw, g1, g2,
+    hf, hs, w, out,
     H, W, acc, DN, A1, A2, X1, X2, Y1, Y2, E, GA, GB, G2, U, T1, R1, T2, R2, V1, V2,
     PA, SA, MA, FA, QA, LA, PB, SB, MB, FB, QB, LB, PG, SG, MG, FG, QG, LG,
     lsem, ssem, rsem,
 ):
     me = Place()
-    net = Net(ssem, rsem)
+    net = Net(me, ssem, rsem)
     own = me.block(0, 0)
+    mine = (me.chip(0, 0), me.c)
     loads = [
-        pltpu.make_async_copy(w, W.at[own], lsem.at[0]),
+        pltpu.make_async_copy(w, W.at[mine], lsem.at[0]),
         pltpu.make_async_copy(hf, H.at[pl.ds(0, ROWS)], lsem.at[1]),
         pltpu.make_async_copy(hs, H.at[pl.ds(ROWS, ROWS)], lsem.at[2]),
     ]
@@ -407,7 +430,7 @@
 
     def project(k, _):
         cols = pl.ds(pl.multiple_of(k * 1024, 1024), 1024)
-        piece = W[pl.ds(8 * k, 8)].reshape(1024, COLS)
+        piece = W[pl.ds(4 * k, 4)].reshape(1024, COLS)
         acc[...] += jnp.dot(H[:, cols], piece, preferred_element_type=F32)
         return 0
 
@@ -422,7 +445,8 @@
         X1[0, 2 * v : 2 * v + 1] = mean
         X1[0, 2 * v + 1 : 2 * v + 2] = jnp.sum(shifted * shifted, axis=0, keepdims=True)
     middle, last = exchange(net, me, X1, X2, merge_moments(ROWS), merge_moments(8 * ROWS))
-    moments = last(middle())
+    middle()
+    moments = last()
     spread = []
     for v, A in ((0, A1), (1, A2)):
         mean = moments[2 * v : 2 * v + 1]
@@ -451,15 +475,18 @@
     gz2.step(0)
     correlate(1)
     correlate(2)
-    columns = middle()
+    middle()
     gz2.step(1)
     correlate(3)
     groups[0].add()
     next(scatter_a)
     correlate(4)
-    sums = last(columns) / TOKENS
+    sums = last() / TOKENS
     E[0, 0:2] = sums[0:2]
-    tops = [net.send(E.at[0], E.at[d], me.up(d)) for d in range(1, NZ)]
+    heads = net.group()
+    heads_by = net.sender(E.at[pl.ds(1, NZ - 1)])
+    for d in range(1, NZ):
+        net.send(E.at[0], E.at[d], me.up(d), heads_by, heads)
     gz2.step(2)
     correlate(5)
     correlate(6)
@@ -483,22 +510,22 @@
                 column = lax.broadcasted_iota(jnp.int32, (32, COLS), 1)
                 same = jnp.logical_and(row < 16, row + 16 * own == column)
                 value = jnp.where(same, diagonal, value)
-            G[own, rows] = value.astype(BF)
-
-    across = []
+            G[mine + (rows,)] = value.astype(BF)
+
+    turned_ref = G2.at[mine + (pl.ds(0, 112),)]
+    turned, turned_by = net.group(), net.sender(turned_ref)
 
     def turn_over(G, group):
         for k in range(4):
             slot = 4 * group + k
             offset = SLOTS[slot]
-            source = G.at[own, pl.ds(16 * k, 16)]
+            source = G.at[mine + (pl.ds(16 * k, 16),)]
             if offset == 0:
-                G2[own, 0:16] = G[own, 0:16]
+                G2[mine + (pl.ds(0, 16),)] = G[mine + (pl.ds(0, 16),)]
             else:
                 there = 7 if offset == 4 else SLOTS.index(-offset)
-                across.append(
-                    net.send(source, G2.at[own, pl.ds(16 * there, 16)], me.up(offset))
-                )
+                target = G2.at[mine + (pl.ds(16 * there, 16),)]
+                net.send(source, target, me.up(offset), turned_by, turned)
 
     finish(scatter_a)
     loss_grad(GA, halves_a, 0)
@@ -506,7 +533,6 @@
     next(gather_a)
     turn_over(GA, 0)
     next(scatter_b)
-    gz1.step(0)
     next(gather_a)
     finish(scatter_b)
     loss_grad(GB, halves_b, 1)
@@ -514,11 +540,11 @@
     next(gather_b)
     turn_over(GB, 1)
     next(gather_a)
+    gz1.step(0)
     next(gather_b)
     next(gather_a)
     gz1.step(1)
-    for copy in tops:
-        copy.wait_recv()
+    net.wait(heads, E.at[pl.ds(1, NZ - 1)])
     for d in range(NZ):
         A1[me.Z(-d), ROWS:PAD] = means(E[d, 0:1])
         A2[me.Z(-d), ROWS:PAD] = means(E[d, 1:2])
@@ -527,8 +553,8 @@
     ones = jnp.ones((16, COLS), BF)
 
     def upstream(A, G, slot, dims, start):
-        rows = pl.ds(16 * (slot % (G.shape[1] // 16)), 16)
-        g = G[:, rows].reshape(COLS, COLS)
+        rows = pl.ds(16 * (slot % (G.shape[2] // 16)), 16)
+        g = G[:, :, rows].reshape(COLS, COLS)
         squares = g * g
         if slot == 0:
             shape = (COLS, COLS)
@@ -555,7 +581,7 @@
 
     def partial(v, T, V, d):
         b = me.Z(d)
-        piece = W[pl.ds(4 * b, 4)].reshape(COLS, COLS)
+        piece = W[pl.ds(2 * b, 2)].reshape(COLS, COLS)
         t = dot(DN[view(v)], piece, ((1,), (1,)))
         if d == 0:
             V[...] = t
@@ -566,16 +592,15 @@
         upstream(A2, GA, slot, (0,), slot == 0)
     next(gather_b)
     gz1.step(2)
-    for copy in across:
-        copy.wait_recv()
+    net.wait(turned, turned_ref)
     gather_2 = gather_plane(net, me, G2)
     next(gather_2)
     finish(gather_b)
     for slot in range(4, 8):
         upstream(A2, GB, slot, (0,), False)
     down(0, A1)
-    ring1 = ScatterZ(net, me, T1, R1, ROWS)
-    ring2 = ScatterZ(net, me, T2, R2, ROWS)
+    ring1 = ScatterZ(net, me, T1, R1)
+    ring2 = ScatterZ(net, me, T2, R2)
     gz1.step(3)
     partial(0, T1, V1, 4)
     ring1.long(0)
@@ -604,13 +629,18 @@
     partial(1, T2, V2, 3)
     partial(1, T2, V2, -3)
     ring2.short(1)
-    weight = Blocks(net, me, PG, SG)
-    for b in range(8):
-        cols = pl.ds(b * COLS, COLS)
-        weight.put(b, dot(H[:, cols], DN[...], ((0,), (0,))))
     partial(1, T2, V2, 2)
     partial(1, T2, V2, -2)
+    weight = Blocks(net, me, PG, SG)
+
+    def weight_block(b):
+        weight.put(b, dot(H[:, pl.ds(b * COLS, COLS)], DN[...], ((0,), (0,))))
+
+    for b in range(5):
+        weight_block(b)
     ring2.long(1)
+    for b in range(5, 8):
+        weight_block(b)
     partial(1, T2, V2, 1)
     partial(1, T2, V2, -1)
     ring2.short(2)
@@ -618,38 +648,38 @@
     scatter_g = scatter_plane(net, me, SG, MG, FG, QG, LG, halves_g)
     weight.add()
     next(scatter_g)
+    partial(1, T2, V2, 0)
     ring2.long(2)
     next(scatter_g)
     ring2.short(3)
-    partial(1, T2, V2, 0)
     next(scatter_g)
     ring2.long(3)
-    for ring, V, out in ((ring1, V1, g1), (ring2, V2, g2)):
-        for half in (0, 1):
-            rows = pl.ds(96 * half, 96)
-            out[rows] = (ring.finish(half) + V[rows]).astype(BF)
+    def writer(start):
+        def write(row, value):
+            out[start + row : start + row + 48] = value.astype(BF)
+
+        return write
+
+    ring1.finish(V1, writer(128))
+    ring2.finish(V2, writer(128 + ROWS))
     finish(scatter_g)
     for o in (0, 1):
-        gw[64 * o : 64 * o + 64] = (halves_g[o] / math.sqrt(TOKENS)).astype(BF)
+        out[64 * o : 64 * o + 64] = (halves_g[o] / math.sqrt(TOKENS)).astype(BF)
     net.drain()
 
 
 def local(hidden_first, hidden_second, weight):
     vm = pl.BlockSpec(memory_space=pltpu.VMEM)
     hbm = pl.BlockSpec(memory_space=pl.ANY)
-    count = 640
-    return pl.pallas_call(
+    senders, count = 27, 253
+    out = pl.pallas_call(
         kernel,
-        out_shape=[
-            jax.ShapeDtypeStruct((128, COLS), BF),
-            jax.ShapeDtypeStruct((ROWS, COLS), BF),
-            jax.ShapeDtypeStruct((ROWS, COLS), BF),
-        ],
+        out_shape=jax.ShapeDtypeStruct((128 + 2 * ROWS, COLS), BF),
         in_specs=[hbm] * 3,
-        out_specs=[vm] * 3,
+        out_specs=vm,
         scratch_shapes=[
             pltpu.VMEM((2 * ROWS, 4096), BF),
-            pltpu.VMEM((32, 128, COLS), BF),
+            pltpu.VMEM((16, 2, 128, COLS), BF),
             pltpu.VMEM((2 * ROWS, COLS), F32),
             pltpu.VMEM((2 * ROWS, COLS), BF),
             pltpu.VMEM((NZ, PAD, COLS), BF),
@@ -659,9 +689,9 @@
             pltpu.VMEM((8, 4, COLS), F32),
             pltpu.VMEM((4, 4, COLS), F32),
             pltpu.VMEM((NZ, 2, COLS), F32),
-            pltpu.VMEM((32, 64, COLS), BF),
-            pltpu.VMEM((32, 64, COLS), BF),
-            pltpu.VMEM((32, 128, COLS), BF),
+            pltpu.VMEM((16, 2, 64, COLS), BF),
+            pltpu.VMEM((16, 2, 64, COLS), BF),
+            pltpu.VMEM((16, 2, 128, COLS), BF),
             pltpu.VMEM((PAD + 8, COLS), F32),
             pltpu.VMEM((NZ, ROWS, COLS), BF),
             pltpu.VMEM((2, 4, ROWS, COLS), BF),
@@ -675,13 +705,14 @@
         + scatter_plane_scratch(128)
         + [
             pltpu.SemaphoreType.DMA((3,)),
-            pltpu.SemaphoreType.DMA((count,)),
+            pltpu.SemaphoreType.DMA((senders,)),
             pltpu.SemaphoreType.DMA((count,)),
         ],
         compiler_params=pltpu.CompilerParams(
             collective_id=1, has_side_effects=True, vmem_limit_bytes=60 * 1024 * 1024
         ),
     )(hidden_first, hidden_second, weight)
+    return out[:128], out[128 : 128 + ROWS], out[128 + ROWS :]
 
 
 def solution(mesh):

time: 144 us -> 137 us (0.951)
  Pallas kernels: 138 us -> 132 us
  local copies, waits for them, and re-layouts: 4.8 us -> 3.36 us
    pallas_call x1, Pallas kernels: 138 us -> 132 us  [local(): pl.pallas_call(kernel, out_shape=jax.ShapeDtypeStruct((128 + 2 * ROWS, CO...]
    unnamed x3 -> x0, local copies, waits for them, and re-layouts: 4.8 us -> none
    slice x0 -> x2, local copies, waits for them, and re-layouts: none -> 3.36 us  [local(): return (out[:128], out[128:128 + ROWS], out[128 + ROWS:])]
where the time goes in v3:
time: 137 us; the launch traced here: 136 us
  Pallas kernels  132 us (96%)
  local copies, waits for them, and re-layouts  3.36 us (2%)
    pallas_call x1, Pallas kernels, local(): pl.pallas_call(kernel, out_shape=jax.ShapeDtypeStruct((128 + 2 * ROWS, CO...  132 us
    slice x2, local copies, waits for them, and re-layouts, local(): return (out[:128], out[128:128 + ROWS], out[128 + ROWS:])  3.36 us

profile of v3, /device:TPU:6, one launch (start us, length us, event | category | flops | bytes accessed | tf_op | source)
XLA Modules:
  0.0 135.6 jit_solution(9123005519023101654)
XLA Ops:
  0.6 131.6 %shard_map.58 = bf16[512,512]{1,0:T(8,128)(2,1)} custom-call(bf16[192,4096]{1,0:T(8,128)(2,1)} %hf.1, bf16[192,4096]{1,0:T(8,128)(2,1)} %hs.1, bf16[128,512]{1,0:T(8,128)(2,1)} %w.1), custom_call_target="tpu_custom_call" | custom-call | tf_op jit(solution)/shard_map/pallas_call | solution.py:675
  132.3 1.8 %fusion = (bf16[192,512]{1,0:T(8,128)(2,1)}, bf16[192,512]{1,0:T(8,128)(2,1)}) fusion(bf16[512,512]{1,0:T(8,128)(2,1)} %shard_map.58), kind=kLoop, calls=%fused_computation | loop fusion | bytes 786432 | tf_op jit(solution)/shard_map/slice | solution.py:715
  134.1 1.6 %slice.9 = bf16[128,512]{1,0:T(8,128)(2,1)} slice(bf16[512,512]{1,0:T(8,128)(2,1)} %shard_map.58), slice={[0:128], [0:512]} | slice | bytes 262144 | tf_op jit(solution)/shard_map/slice | solution.py:715

commit v4 on v3

--- a/solution.py
+++ b/solution.py
@@ -123,6 +123,11 @@
 def finish(steps):
     for _ in steps:
         pass
+
+
+def advance(steps, count):
+    for _ in range(count):
+        next(steps)
 
 
 def gather_plane(net, me, W):
@@ -174,7 +179,7 @@
             push(block(o, a, -d), start, quarter, to(o, 0, d), far[k])
         for o, d in both:
             share(o, a, -d)
-    yield
+        yield
     for k, a in enumerate((0, -1, 1, -2)):
         net.wait(far[k], block_ref)
         for o in (0, 1):
@@ -388,9 +393,9 @@
         for d, piece in self.order():
             self.send(0, d, piece)
 
-    def step(self, s):
+    def step(self, s, places=range(8)):
         for place, (d, piece) in enumerate(self.order()):
-            if (s, d, piece) in self.copies:
+            if place in places and (s, d, piece) in self.copies:
                 self.copies[s, d, piece].wait_recv()
                 if s < 2 or (s == 2 and place < 4):
                     self.send(s + 1, d, piece)
@@ -405,7 +410,7 @@
 
 def kernel(
     hf, hs, w, out,
-    H, W, acc, DN, A1, A2, X1, X2, Y1, Y2, E, GA, GB, G2, U, T1, R1, T2, R2, V1, V2,
+    H, W, acc, DN, A1, A2, B1, B2, X1, X2, Y1, Y2, E, E2, GA, GB, G2, U, T1, R1, T2, R2, V1, V2, PF,
     PA, SA, MA, FA, QA, LA, PB, SB, MB, FB, QB, LB, PG, SG, MG, FG, QG, LG,
     lsem, ssem, rsem,
 ):
@@ -439,23 +444,40 @@
     def view(v):
         return slice(v * ROWS, (v + 1) * ROWS)
 
-    for v in range(2):
+    local_mean = []
+    for v, B in ((0, B1), (1, B2)):
         mean = jnp.sum(acc[view(v)], axis=0, keepdims=True) / ROWS
         shifted = acc[view(v)] - mean
         X1[0, 2 * v : 2 * v + 1] = mean
         X1[0, 2 * v + 1 : 2 * v + 2] = jnp.sum(shifted * shifted, axis=0, keepdims=True)
+        B[me.z] = shifted.astype(BF)
+        local_mean.append(mean)
+    gz2 = GatherZ(net, me, B2)
+    gz1 = GatherZ(net, me, B1)
     middle, last = exchange(net, me, X1, X2, merge_moments(ROWS), merge_moments(8 * ROWS))
+    gz2.start()
     middle()
+    gz2.step(0)
     moments = last()
-    spread = []
-    for v, A in ((0, A1), (1, A2)):
-        mean = moments[2 * v : 2 * v + 1]
+    spread, moves = [], []
+    for v in range(2):
         spread.append(jnp.sqrt(moments[2 * v + 1 : 2 * v + 2] / TOKENS + epsilon))
-        A[me.z, 0:ROWS] = ((acc[view(v)] - mean) / spread[v]).astype(BF)
-
-    gz2 = GatherZ(net, me, A2)
-    gz1 = GatherZ(net, me, A1)
-    gz2.start()
+        moves.append((local_mean[v] - moments[2 * v : 2 * v + 1], 1.0 / spread[v]))
+    E2[0] = jnp.concatenate(moves[1], axis=0)
+    scales, scales_by = net.group(), net.sender(E2.at[pl.ds(1, NZ - 1)])
+    for d in range(1, NZ):
+        net.send(E2.at[0], E2.at[d], me.up(d), scales_by, scales)
+
+    def normalize(A, B, offset, move, scale):
+        b = me.Z(offset)
+        A[b, 0:ROWS] = ((B[b].astype(F32) + move) * scale).astype(BF)
+
+    def normalize2(slot):
+        d = -SLOTS[slot] % NZ
+        normalize(A2, B2, SLOTS[slot], E2[d, 0:1], E2[d, 1:2])
+
+    normalize(A1, B1, 0, *moves[0])
+    normalize(A2, B2, 0, *moves[1])
     n1, n2 = A1[me.z, 0:ROWS].astype(F32), A2[me.z, 0:ROWS].astype(F32)
     Y1[0, 0:1] = jnp.sum(n1, axis=0, keepdims=True)
     Y1[0, 1:2] = jnp.sum(n2, axis=0, keepdims=True)
@@ -465,29 +487,34 @@
     groups = (Pairs(net, me, PA, SA), Pairs(net, me, PB, SB))
 
     def correlate(slot):
+        if slot > 0:
+            normalize2(slot)
         value = dot(A2[me.Z(SLOTS[slot]), 0:ROWS], A1[me.z, 0:ROWS], ((0,), (0,)))
         groups[slot // 4].put(slot % 4, value)
 
     halves_a, halves_b = [], []
     scatter_a = scatter_plane(net, me, SA, MA, FA, QA, LA, halves_a)
     scatter_b = scatter_plane(net, me, SB, MB, FB, QB, LB, halves_b)
+    gz2.step(1, range(4))
     correlate(0)
-    gz2.step(0)
+    gz2.step(1, range(4, 8))
+    net.wait(scales, E2.at[pl.ds(1, NZ - 1)])
     correlate(1)
     correlate(2)
     middle()
-    gz2.step(1)
+    gz2.step(2, range(4))
     correlate(3)
     groups[0].add()
     next(scatter_a)
     correlate(4)
     sums = last() / TOKENS
     E[0, 0:2] = sums[0:2]
+    E[0, 2:4] = jnp.concatenate(moves[0], axis=0)
     heads = net.group()
     heads_by = net.sender(E.at[pl.ds(1, NZ - 1)])
     for d in range(1, NZ):
         net.send(E.at[0], E.at[d], me.up(d), heads_by, heads)
-    gz2.step(2)
+    gz2.step(2, range(4, 8))
     correlate(5)
     correlate(6)
     next(scatter_a)
@@ -498,7 +525,7 @@
     next(scatter_b)
     next(scatter_a)
     next(scatter_b)
-
+    gz1.step(0)
     diagonal = 2.0 * (sums[2:3] - 1.0)
 
     def loss_grad(G, halves, group):
@@ -539,16 +566,19 @@
     gather_b = gather_plane(net, me, GB)
     next(gather_b)
     turn_over(GB, 1)
-    next(gather_a)
-    gz1.step(0)
+    gz1.step(1)
+    advance(gather_a, 4)
     next(gather_b)
     next(gather_a)
-    gz1.step(1)
     net.wait(heads, E.at[pl.ds(1, NZ - 1)])
     for d in range(NZ):
         A1[me.Z(-d), ROWS:PAD] = means(E[d, 0:1])
         A2[me.Z(-d), ROWS:PAD] = means(E[d, 1:2])
-    next(gather_b)
+    advance(gather_b, 4)
+    net.wait(turned, turned_ref)
+    gather_2 = gather_plane(net, me, G2)
+    next(gather_2)
+    gz1.step(2)
     finish(gather_a)
     ones = jnp.ones((16, COLS), BF)
 
@@ -591,9 +621,6 @@
     for slot in range(4):
         upstream(A2, GA, slot, (0,), slot == 0)
     next(gather_b)
-    gz1.step(2)
-    net.wait(turned, turned_ref)
-    gather_2 = gather_plane(net, me, G2)
     next(gather_2)
     finish(gather_b)
     for slot in range(4, 8):
@@ -601,7 +628,10 @@
     down(0, A1)
     ring1 = ScatterZ(net, me, T1, R1)
     ring2 = ScatterZ(net, me, T2, R2)
-    gz1.step(3)
+
+    def weight_first(b):
+        PF[b] = dot(H[0:ROWS, pl.ds(b * COLS, COLS)], DN[0:ROWS], ((0,), (0,)))
+
     partial(0, T1, V1, 4)
     ring1.long(0)
     partial(0, T1, V1, 3)
@@ -610,17 +640,31 @@
     next(gather_2)
     partial(0, T1, V1, 2)
     partial(0, T1, V1, -2)
+    gz1.step(3)
+    next(gather_2)
+    weight_first(0)
+    weight_first(1)
     ring1.long(1)
-    ring1.short(2)
+    next(gather_2)
     partial(0, T1, V1, 1)
     partial(0, T1, V1, -1)
+    ring1.short(2)
     next(gather_2)
+    weight_first(2)
+    weight_first(3)
+    partial(0, T1, V1, 0)
     ring1.long(2)
+    weight_first(4)
+    weight_first(5)
+    next(gather_2)
     ring1.short(3)
-    partial(0, T1, V1, 0)
-    next(gather_2)
+    weight_first(6)
+    weight_first(7)
     ring1.long(3)
     finish(gather_2)
+    for slot in range(1, 8):
+        d = -SLOTS[slot] % NZ
+        normalize(A1, B1, SLOTS[slot], E[d, 2:3], E[d, 3:4])
     for slot in range(8):
         upstream(A1, G2, slot, (1,), slot == 0)
     down(1, A2)
@@ -629,30 +673,26 @@
     partial(1, T2, V2, 3)
     partial(1, T2, V2, -3)
     ring2.short(1)
+    weight = Blocks(net, me, PG, SG)
+    for b in range(8):
+        second = dot(
+            H[ROWS : 2 * ROWS, pl.ds(b * COLS, COLS)], DN[ROWS : 2 * ROWS], ((0,), (0,))
+        )
+        weight.put(b, PF[b] + second)
     partial(1, T2, V2, 2)
     partial(1, T2, V2, -2)
-    weight = Blocks(net, me, PG, SG)
-
-    def weight_block(b):
-        weight.put(b, dot(H[:, pl.ds(b * COLS, COLS)], DN[...], ((0,), (0,))))
-
-    for b in range(5):
-        weight_block(b)
     ring2.long(1)
-    for b in range(5, 8):
-        weight_block(b)
-    partial(1, T2, V2, 1)
-    partial(1, T2, V2, -1)
-    ring2.short(2)
     halves_g = []
     scatter_g = scatter_plane(net, me, SG, MG, FG, QG, LG, halves_g)
     weight.add()
     next(scatter_g)
+    partial(1, T2, V2, 1)
+    partial(1, T2, V2, -1)
+    ring2.short(2)
     partial(1, T2, V2, 0)
     ring2.long(2)
     next(scatter_g)
     ring2.short(3)
-    next(scatter_g)
     ring2.long(3)
     def writer(start):
         def write(row, value):
@@ -661,6 +701,7 @@
         return write
 
     ring1.finish(V1, writer(128))
+    next(scatter_g)
     ring2.finish(V2, writer(128 + ROWS))
     finish(scatter_g)
     for o in (0, 1):
@@ -671,7 +712,7 @@
 def local(hidden_first, hidden_second, weight):
     vm = pl.BlockSpec(memory_space=pltpu.VMEM)
     hbm = pl.BlockSpec(memory_space=pl.ANY)
-    senders, count = 27, 253
+    senders, count = 28, 254
     out = pl.pallas_call(
         kernel,
         out_shape=jax.ShapeDtypeStruct((128 + 2 * ROWS, COLS), BF),
@@ -684,10 +725,13 @@
             pltpu.VMEM((2 * ROWS, COLS), BF),
             pltpu.VMEM((NZ, PAD, COLS), BF),
             pltpu.VMEM((NZ, PAD, COLS), BF),
+            pltpu.VMEM((NZ, ROWS, COLS), BF),
+            pltpu.VMEM((NZ, ROWS, COLS), BF),
             pltpu.VMEM((8, 4, COLS), F32),
             pltpu.VMEM((4, 4, COLS), F32),
             pltpu.VMEM((8, 4, COLS), F32),
             pltpu.VMEM((4, 4, COLS), F32),
+            pltpu.VMEM((NZ, 4, COLS), F32),
             pltpu.VMEM((NZ, 2, COLS), F32),
             pltpu.VMEM((16, 2, 64, COLS), BF),
             pltpu.VMEM((16, 2, 64, COLS), BF),
@@ -699,6 +743,7 @@
             pltpu.VMEM((2, 4, ROWS, COLS), BF),
             pltpu.VMEM((ROWS, COLS), F32),
             pltpu.VMEM((ROWS, COLS), F32),
+            pltpu.VMEM((8, COLS, COLS), F32),
         ]
         + scatter_plane_scratch(64)
         + scatter_plane_scratch(64)

time: 137 us -> 126 us (0.920)
  Pallas kernels: 132 us -> 121 us
    pallas_call x1, Pallas kernels: 132 us -> 121 us  [local(): pl.pallas_call(kernel, out_shape=jax.ShapeDtypeStruct((128 + 2 * ROWS, CO...]
where the time goes in v4:
time: 126 us; the launch traced here: 125 us
  Pallas kernels  121 us (96%)
  local copies, waits for them, and re-layouts  3.36 us (3%)
    pallas_call x1, Pallas kernels, local(): pl.pallas_call(kernel, out_shape=jax.ShapeDtypeStruct((128 + 2 * ROWS, CO...  121 us
    slice x2, local copies, waits for them, and re-layouts, local(): return (out[:128], out[128:128 + ROWS], out[128 + ROWS:])  3.36 us

profile of v4, /device:TPU:6, one launch (start us, length us, event | category | flops | bytes accessed | tf_op | source)
XLA Modules:
  0.0 124.7 jit_solution(5136338536513927049)
XLA Ops:
  0.6 120.7 %shard_map.58 = bf16[512,512]{1,0:T(8,128)(2,1)} custom-call(bf16[192,4096]{1,0:T(8,128)(2,1)} %hf.1, bf16[192,4096]{1,0:T(8,128)(2,1)} %hs.1, bf16[128,512]{1,0:T(8,128)(2,1)} %w.1), custom_call_target="tpu_custom_call" | custom-call | tf_op jit(solution)/shard_map/pallas_call | solution.py:716
  121.4 1.8 %fusion = (bf16[192,512]{1,0:T(8,128)(2,1)}, bf16[192,512]{1,0:T(8,128)(2,1)}) fusion(bf16[512,512]{1,0:T(8,128)(2,1)} %shard_map.58), kind=kLoop, calls=%fused_computation | loop fusion | bytes 786432 | tf_op jit(solution)/shard_map/slice | solution.py:760
  123.2 1.6 %slice.9 = bf16[128,512]{1,0:T(8,128)(2,1)} slice(bf16[512,512]{1,0:T(8,128)(2,1)} %shard_map.58), slice={[0:128], [0:512]} | slice | bytes 262144 | tf_op jit(solution)/shard_map/slice | solution.py:760

commit v5 on v4

--- a/solution.py
+++ b/solution.py
@@ -46,9 +46,6 @@
 
     def block(self, dx, dy, dc=0):
         return self.X(dx) * 8 + self.Y(dy) * 2 + wrap(self.c + dc, 2)
-
-    def chip(self, dx, dy):
-        return self.X(dx) * 4 + self.Y(dy)
 
     def at(self, dx, dy, dc=0):
         return {"dp": self.block(dx, dy, dc)}
@@ -131,61 +128,60 @@
 
 
 def gather_plane(net, me, W):
-    rows = W.shape[2]
+    rows = W.shape[3]
     part, quarter = rows // 2, rows // 4
 
     def block(o, a, b):
-        return me.chip(*turn(o, a, b))
+        da, db = turn(o, a, b)
+        return me.X(da), me.Y(db)
 
     def to(o, a, b):
         return me.at(*turn(o, a, b))
 
-    def push(index, start, size, target, group=None):
-        ref = W.at[index, me.c, pl.ds(start, size)]
-        return net.send(ref, ref, target, many, group)
-
-    own = me.chip(0, 0)
-    block_ref = W.at[own, me.c]
+    def push(index, start, size, target, sender, group=None):
+        ref = W.at[index + (me.c, pl.ds(start, size))]
+        return net.send(ref, ref, target, sender, group)
+
+    own = (me.X(0), me.Y(0))
+    block_ref = W.at[own + (me.c,)]
     both = [(o, d) for d in (1, -1) for o in (0, 1)]
     first, second = {}, {}
     shared, far = net.group(), [net.group() for _ in range(4)]
-    many, one = net.sender(W.at[pl.ds(0, 15)]), net.sender(block_ref)
+    by_first, by_second = net.sender(W.at[0, pl.ds(0, 3), 0]), net.sender(W.at[0])
+    by_far, by_shared = net.sender(W.at[0, pl.ds(0, 2)]), net.sender(W.at[:, :, 0])
 
     def over(o, a):
         for d in (1, -1):
-            second[o, a, d] = push(block(o, a, 0), part * o, part, to(o, 0, d))
-
-    def share(o, a, b):
-        push(block(o, a, b), part * o, part, me.sib(), shared)
+            second[o, a, d] = push(block(o, a, 0), part * o, part, to(o, 0, d), by_second)
+
+    def share(o, a):
+        line = (me.X(a), slice(None)) if o == 0 else (slice(None), me.Y(a))
+        ref = W.at[line + (me.c, pl.ds(part * o, part))]
+        net.send(ref, ref, me.sib(), by_shared, shared)
 
     for d in (1, -1, 2):
         for o in (0, 1):
-            first[o, d] = push(own, part * o, part, to(o, d, 0))
+            first[o, d] = push(own, part * o, part, to(o, d, 0), by_first)
     for o in (0, 1):
         over(o, 0)
-    net.send(block_ref, block_ref, me.sib(), one, shared)
     yield
     for d in (1, -1, 2):
         for o in (0, 1):
             first[o, d].wait_recv()
             over(o, -d)
-        for o in (0, 1):
-            share(o, -d, 0)
     yield
     for k, a in enumerate((0, -1, 1, -2)):
         for o, d in both:
             second[o, a, d].wait_recv()
             start = part * o + (0 if d == 1 else quarter)
-            push(block(o, a, -d), start, quarter, to(o, 0, d), far[k])
-        for o, d in both:
-            share(o, a, -d)
+            push(block(o, a, -d), start, quarter, to(o, 0, d), by_far, far[k])
         yield
     for k, a in enumerate((0, -1, 1, -2)):
         net.wait(far[k], block_ref)
         for o in (0, 1):
-            share(o, a, 2)
+            share(o, a)
     yield
-    net.wait(shared, W.at[:, 1 - me.c])
+    net.wait(shared, W.at[:, :, 1 - me.c])
 
 
 def scatter_plane(net, me, S, M1, F1, Q, F2, result):
@@ -417,7 +413,7 @@
     me = Place()
     net = Net(me, ssem, rsem)
     own = me.block(0, 0)
-    mine = (me.chip(0, 0), me.c)
+    mine = (me.x, me.y, me.c)
     loads = [
         pltpu.make_async_copy(w, W.at[mine], lsem.at[0]),
         pltpu.make_async_copy(hf, H.at[pl.ds(0, ROWS)], lsem.at[1]),
@@ -435,7 +431,7 @@
 
     def project(k, _):
         cols = pl.ds(pl.multiple_of(k * 1024, 1024), 1024)
-        piece = W[pl.ds(4 * k, 4)].reshape(1024, COLS)
+        piece = W[k].reshape(1024, COLS)
         acc[...] += jnp.dot(H[:, cols], piece, preferred_element_type=F32)
         return 0
 
@@ -583,8 +579,8 @@
     ones = jnp.ones((16, COLS), BF)
 
     def upstream(A, G, slot, dims, start):
-        rows = pl.ds(16 * (slot % (G.shape[2] // 16)), 16)
-        g = G[:, :, rows].reshape(COLS, COLS)
+        rows = pl.ds(16 * (slot % (G.shape[3] // 16)), 16)
+        g = G[:, :, :, rows].reshape(COLS, COLS)
         squares = g * g
         if slot == 0:
             shape = (COLS, COLS)
@@ -611,7 +607,7 @@
 
     def partial(v, T, V, d):
         b = me.Z(d)
-        piece = W[pl.ds(2 * b, 2)].reshape(COLS, COLS)
+        piece = W[lax.div(b, 2), pl.ds(2 * lax.rem(b, 2), 2)].reshape(COLS, COLS)
         t = dot(DN[view(v)], piece, ((1,), (1,)))
         if d == 0:
             V[...] = t
@@ -656,15 +652,15 @@
     ring1.long(2)
     weight_first(4)
     weight_first(5)
+    for slot in range(1, 8):
+        d = -SLOTS[slot] % NZ
+        normalize(A1, B1, SLOTS[slot], E[d, 2:3], E[d, 3:4])
     next(gather_2)
     ring1.short(3)
     weight_first(6)
     weight_first(7)
     ring1.long(3)
     finish(gather_2)
-    for slot in range(1, 8):
-        d = -SLOTS[slot] % NZ
-        normalize(A1, B1, SLOTS[slot], E[d, 2:3], E[d, 3:4])
     for slot in range(8):
         upstream(A1, G2, slot, (1,), slot == 0)
     down(1, A2)
@@ -712,7 +708,7 @@
 def local(hidden_first, hidden_second, weight):
     vm = pl.BlockSpec(memory_space=pltpu.VMEM)
     hbm = pl.BlockSpec(memory_space=pl.ANY)
-    senders, count = 28, 254
+    senders, count = 36, 254
     out = pl.pallas_call(
         kernel,
         out_shape=jax.ShapeDtypeStruct((128 + 2 * ROWS, COLS), BF),
@@ -720,7 +716,7 @@
         out_specs=vm,
         scratch_shapes=[
             pltpu.VMEM((2 * ROWS, 4096), BF),
-            pltpu.VMEM((16, 2, 128, COLS), BF),
+            pltpu.VMEM((4, 4, 2, 128, COLS), BF),
             pltpu.VMEM((2 * ROWS, COLS), F32),
             pltpu.VMEM((2 * ROWS, COLS), BF),
             pltpu.VMEM((NZ, PAD, COLS), BF),
@@ -733,9 +729,9 @@
             pltpu.VMEM((4, 4, COLS), F32),
             pltpu.VMEM((NZ, 4, COLS), F32),
             pltpu.VMEM((NZ, 2, COLS), F32),
-            pltpu.VMEM((16, 2, 64, COLS), BF),
-            pltpu.VMEM((16, 2, 64, COLS), BF),
-            pltpu.VMEM((16, 2, 128, COLS), BF),
+            pltpu.VMEM((4, 4, 2, 64, COLS), BF),
+            pltpu.VMEM((4, 4, 2, 64, COLS), BF),
+            pltpu.VMEM((4, 4, 2, 128, COLS), BF),
             pltpu.VMEM((PAD + 8, COLS), F32),
             pltpu.VMEM((NZ, ROWS, COLS), BF),
             pltpu.VMEM((2, 4, ROWS, COLS), BF),

time: 126 us -> 127 us (level)
  no operation moved by 1% of the time
where the time goes in v5:
time: 127 us; the launch traced here: 125 us
  Pallas kernels  121 us (95%)
  local copies, waits for them, and re-layouts  3.36 us (3%)
    pallas_call x1, Pallas kernels, local(): pl.pallas_call(kernel, out_shape=jax.ShapeDtypeStruct((128 + 2 * ROWS, CO...  121 us
    slice x2, local copies, waits for them, and re-layouts, local(): return (out[:128], out[128:128 + ROWS], out[128 + ROWS:])  3.36 us

profile of v5, /device:TPU:6, one launch (start us, length us, event | category | flops | bytes accessed | tf_op | source)
XLA Modules:
  0.0 124.9 jit_solution(14566939307237367233)
XLA Ops:
  0.6 120.9 %shard_map.58 = bf16[512,512]{1,0:T(8,128)(2,1)} custom-call(bf16[192,4096]{1,0:T(8,128)(2,1)} %hf.1, bf16[192,4096]{1,0:T(8,128)(2,1)} %hs.1, bf16[128,512]{1,0:T(8,128)(2,1)} %w.1), custom_call_target="tpu_custom_call" | custom-call | tf_op jit(solution)/shard_map/pallas_call | solution.py:712
  121.5 1.8 %fusion = (bf16[192,512]{1,0:T(8,128)(2,1)}, bf16[192,512]{1,0:T(8,128)(2,1)}) fusion(bf16[512,512]{1,0:T(8,128)(2,1)} %shard_map.58), kind=kLoop, calls=%fused_computation | loop fusion | bytes 786432 | tf_op jit(solution)/shard_map/slice | solution.py:756
  123.3 1.6 %slice.9 = bf16[128,512]{1,0:T(8,128)(2,1)} slice(bf16[512,512]{1,0:T(8,128)(2,1)} %shard_map.58), slice={[0:128], [0:512]} | slice | bytes 262144 | tf_op jit(solution)/shard_map/slice | solution.py:756

commit v6 on v5

--- a/solution.py
+++ b/solution.py
@@ -521,7 +521,6 @@
     next(scatter_b)
     next(scatter_a)
     next(scatter_b)
-    gz1.step(0)
     diagonal = 2.0 * (sums[2:3] - 1.0)
 
     def loss_grad(G, halves, group):
@@ -555,6 +554,7 @@
     gather_a = gather_plane(net, me, GA)
     next(gather_a)
     turn_over(GA, 0)
+    gz1.step(0)
     next(scatter_b)
     next(gather_a)
     finish(scatter_b)
@@ -664,40 +664,41 @@
     for slot in range(8):
         upstream(A1, G2, slot, (1,), slot == 0)
     down(1, A2)
+    def writer(start):
+        def write(row, value):
+            out[start + row : start + row + 48] = value.astype(BF)
+
+        return write
+
     partial(1, T2, V2, 4)
     ring2.long(0)
-    partial(1, T2, V2, 3)
-    partial(1, T2, V2, -3)
-    ring2.short(1)
     weight = Blocks(net, me, PG, SG)
     for b in range(8):
         second = dot(
             H[ROWS : 2 * ROWS, pl.ds(b * COLS, COLS)], DN[ROWS : 2 * ROWS], ((0,), (0,))
         )
         weight.put(b, PF[b] + second)
+        if b == 3:
+            partial(1, T2, V2, 3)
+            partial(1, T2, V2, -3)
+            ring2.short(1)
+    weight.add()
+    halves_g = []
+    scatter_g = scatter_plane(net, me, SG, MG, FG, QG, LG, halves_g)
+    next(scatter_g)
     partial(1, T2, V2, 2)
     partial(1, T2, V2, -2)
     ring2.long(1)
-    halves_g = []
-    scatter_g = scatter_plane(net, me, SG, MG, FG, QG, LG, halves_g)
-    weight.add()
-    next(scatter_g)
     partial(1, T2, V2, 1)
     partial(1, T2, V2, -1)
     ring2.short(2)
+    next(scatter_g)
     partial(1, T2, V2, 0)
     ring2.long(2)
+    ring1.finish(V1, writer(128))
+    ring2.short(3)
     next(scatter_g)
-    ring2.short(3)
     ring2.long(3)
-    def writer(start):
-        def write(row, value):
-            out[start + row : start + row + 48] = value.astype(BF)
-
-        return write
-
-    ring1.finish(V1, writer(128))
-    next(scatter_g)
     ring2.finish(V2, writer(128 + ROWS))
     finish(scatter_g)
     for o in (0, 1):

time: 127 us -> 125 us (0.984)
  no operation moved by 1% of the time
where the time goes in v6:
time: 125 us; the launch traced here: 124 us
  Pallas kernels  120 us (96%)
  local copies, waits for them, and re-layouts  3.36 us (3%)
    pallas_call x1, Pallas kernels, local(): pl.pallas_call(kernel, out_shape=jax.ShapeDtypeStruct((128 + 2 * ROWS, CO...  120 us
    slice x2, local copies, waits for them, and re-layouts, local(): return (out[:128], out[128:128 + ROWS], out[128 + ROWS:])  3.36 us

profile of v6, /device:TPU:6, one launch (start us, length us, event | category | flops | bytes accessed | tf_op | source)
XLA Modules:
  0.0 124.1 jit_solution(13963919077137661751)
XLA Ops:
  0.6 120.1 %shard_map.58 = bf16[512,512]{1,0:T(8,128)(2,1)} custom-call(bf16[192,4096]{1,0:T(8,128)(2,1)} %hf.1, bf16[192,4096]{1,0:T(8,128)(2,1)} %hs.1, bf16[128,512]{1,0:T(8,128)(2,1)} %w.1), custom_call_target="tpu_custom_call" | custom-call | tf_op jit(solution)/shard_map/pallas_call | solution.py:713
  120.7 1.8 %fusion = (bf16[192,512]{1,0:T(8,128)(2,1)}, bf16[192,512]{1,0:T(8,128)(2,1)}) fusion(bf16[512,512]{1,0:T(8,128)(2,1)} %shard_map.58), kind=kLoop, calls=%fused_computation | loop fusion | bytes 786432 | tf_op jit(solution)/shard_map/slice | solution.py:757
  122.5 1.6 %slice.9 = bf16[128,512]{1,0:T(8,128)(2,1)} slice(bf16[512,512]{1,0:T(8,128)(2,1)} %shard_map.58), slice={[0:128], [0:512]} | slice | bytes 262144 | tf_op jit(solution)/shard_map/slice | solution.py:757
